TPU v7x, 32 devices: a whole 2x2x4 slice. The times are simulated.
32 devices in a mesh: rec: 2 (over x), tm: 16 (over z, y, core).
Axes of the slice: x: 2, y: 2, z: 4, core: 2. Of those that a mesh axis runs over, the one named last changes fastest.
Arguments:
- raw: bfloat16 [2048, 6144], P(('rec', 'tm')), parts along dimension 0, may hold values from -8.5 to 8.5
- pole: float32 [6144], replicated, may hold values from 0.96 to 1, as said below
- order: int32 [96, 64], replicated, may hold values from 0 to 63, each once within a row
- templates: bfloat16 [1152, 61, 32], replicated, may hold values from -0.125 to 0.125
- support: int32 [1152, 32], replicated, may hold values 0 or 1
Outputs:
- scores: bfloat16 [2048, 1152], P(('rec', 'tm')), parts along dimension 0
- whitening: float32 [384, 32, 32], P('rec'), parts along dimension 0
There are 2 independent parts, one for each index of `rec`. A program takes and returns all parts, laid end to end along the dimension named above; an argument that names none is the same for every part. Nothing has to cross between parts.
Inputs may be any that keep to these rules, and one draw needn't show every extreme that they name: Each channel's pole lies in this range. Each row of order is a permutation of 0 to 63.
All inputs are finite; a program needn't handle non-finite values.
Results may differ from a plain program's by a relative error of at most 0.0075.
Values may be sent and summed in bfloat16 or wider, within the bound.
No kernel may reach another device: no remote copies, remote signals or barrier semaphores. Data moves between devices by JAX's collectives and lax.ppermute only.
A program may use at most 128 MiB of HBM per device.

v0:
```python
import jax
import jax.numpy as jnp
from jax import lax
from jax.sharding import PartitionSpec as P

NB = 32
TAPS = 61
NS_ITERS = 4


RIDGE = 0.1


def passed_along(block, axis, distance):
    devices = range(lax.axis_size(axis))
    route = [(i - distance, i) for i in devices if i - distance in devices]
    return lax.ppermute(block, axis, route)


def prefix(value, axis, join, neutral):
    count, mine = (lax.axis_size(axis), lax.axis_index(axis))
    pieces = jax.tree.map(lambda part: lax.all_gather(part, axis), value)
    running = jax.tree.map(
        lambda part, zero: jnp.full_like(part, 0) + jnp.asarray(zero, part.dtype), value, neutral
    )

    def lap(position, running):
        longer = join(running, jax.tree.map(lambda part: part[position], pieces))
        return jax.tree.map(lambda new, old: jnp.where(position < mine, new, old), longer, running)

    return lax.fori_loop(0, count - 1, lap, running)


def compose(earlier, later):
    return (earlier[0] * later[0], earlier[1] * later[0] + later[1])


def root_inverse(covariance):
    width = covariance.shape[-1]
    identity = jnp.eye(width, dtype=jnp.float32)
    traces = jnp.trace(covariance, axis1=1, axis2=2)
    shifted = covariance + (RIDGE * traces / width)[:, None, None] * identity
    norms = jnp.sqrt(jnp.sum(shifted * shifted, axis=(1, 2)))
    estimate = shifted / norms[:, None, None]
    inverse = jnp.broadcast_to(identity, shifted.shape)
    for repeat in range(NS_ITERS):
        middle = 1.5 * identity - 0.5 * jnp.einsum(
            "gij,gjk->gik", inverse, estimate, precision=lax.Precision.HIGHEST
        )
        estimate = jnp.einsum("gij,gjk->gik", estimate, middle, precision=lax.Precision.HIGHEST)
        inverse = jnp.einsum("gij,gjk->gik", middle, inverse, precision=lax.Precision.HIGHEST)
    return inverse / jnp.sqrt(norms)[:, None, None]


def whiten_rows_local(grouped, whitening):
    result = jnp.einsum(
        "tgk,gjk->tgj", grouped.astype(jnp.float32), whitening, precision=lax.Precision.HIGHEST
    )
    return result.astype(jnp.bfloat16).reshape(
        grouped.shape[0], grouped.shape[1] * grouped.shape[2]
    )


def local(raw, pole, order, templates, support):
    row_count, n_chan = raw.shape
    devices = lax.axis_size("tm")
    n_groups = n_chan // NB
    channel_ids = (order + 64 * jnp.arange(order.shape[0], dtype=jnp.int32)[:, None]).reshape(-1)
    half_sum = 0.5 * (1.0 + pole)
    before = passed_along(raw[-1:], "tm", 1)
    current = raw.astype(jnp.float32)
    earlier = jnp.concatenate([before, raw[:-1]], axis=0).astype(jnp.float32)
    drive = half_sum * (current - earlier)
    block_count = row_count // 16
    blocked = drive.reshape(block_count, 16, n_chan)
    level = jnp.zeros((block_count, n_chan), jnp.float32)
    factor = jnp.ones_like(pole)
    within_list = []
    factor_list = []
    for offset in range(16):
        level = pole * level + blocked[:, offset]
        within_list.append(level)
        factor = factor * pole
        factor_list.append(factor)
    within = jnp.stack(within_list, axis=1)
    factors = jnp.stack(factor_list, axis=0)
    ends = within[:, -1]
    spans = jnp.broadcast_to(factors[-1], ends.shape)
    block_powers, block_states = lax.associative_scan(compose, (spans, ends))
    entering = jnp.concatenate([jnp.zeros((1, n_chan), jnp.float32), block_states[:-1]], axis=0)
    offsets = jnp.concatenate([jnp.ones((1, n_chan), jnp.float32), block_powers[:-1]], axis=0)
    shard_power = block_powers[-1]
    shard_state = block_states[-1]
    unused, incoming = prefix(
        (shard_power, shard_state), "tm", compose, (jnp.ones_like(pole), jnp.zeros_like(pole))
    )
    filtered = (
        within + factors[None] * entering[:, None] + offsets[:, None] * factors[None] * incoming
    )
    stored = filtered.reshape(row_count, n_chan).astype(jnp.bfloat16)
    grouped = stored[:, channel_ids].reshape(row_count, n_groups, NB)
    partial_sum = jnp.einsum("tgj,tgk->gjk", grouped, grouped, preferred_element_type=jnp.float32)
    total_t = row_count * devices
    covariance = lax.psum(partial_sum, "tm") / total_t
    whitening = root_inverse(covariance)
    white = whiten_rows_local(grouped, whitening)
    following = passed_along(white[: TAPS - 1], "tm", -1)
    extended = jnp.concatenate([white, following], axis=0)
    kernel = (templates * support[:, None, :].astype(jnp.bfloat16)).transpose(1, 2, 0)
    scores = lax.conv_general_dilated(
        extended[None],
        kernel,
        (1,),
        "VALID",
        dimension_numbers=("NWC", "WIO", "NWC"),
        feature_group_count=n_groups,
        preferred_element_type=jnp.float32,
    )[0]
    return (scores.astype(jnp.bfloat16), whitening)


def solution(mesh):
    in_specs = (P(("rec", "tm"), None), P(), P(), P(), P())
    out_specs = (P(("rec", "tm"), None), P("rec", None, None))
    return jax.shard_map(local, mesh=mesh, in_specs=in_specs, out_specs=out_specs, check_vma=False)
```

profile of v0, /device:TPU:0, one launch (start us, length us, event | category | flops | bytes accessed | tf_op | source)
XLA Modules:
  0.0 755.4 jit_solution(1984602462439454194)
XLA Ops:
  8.1 2.4 collective-permute-start
  16.9 1.8 subtract_multiply_fusion
  25.7 2.1 pad.31
  27.8 2.1 pad.35
  32.6 23.7 %all-gather.1 = f32[16,1,6144]{2,1,0:T(1,128)S(1)} all-gather(f32[1,1,6144]{2,1,0:T(1,128)S(1)} %get-tuple-element.176), channel_id=1, replica_groups=mesh['rec'=2,'tm'=16] {'tm'}, dimensions={0}, use_global_device_ids=true | all-gather | bytes 417792 | tf_op jit(solution)/shard_map/all_gather | solution.py:22
  57.2 18.5 %all-gather = f32[16,1,6144]{2,1,0:T(1,128)S(1)} all-gather(f32[1,1,6144]{2,1,0:T(1,128)S(1)} %get-tuple-element.177), channel_id=1, replica_groups=mesh['rec'=2,'tm'=16] {'tm'}, dimensions={0}, use_global_device_ids=true | all-gather | bytes 417792 | tf_op jit(solution)/shard_map/all_gather | solution.py:22
  76.5 16.7 %while.14 = (s32[]{:T(128)}, f32[6144]{0:T(1024)S(1)}, s32[]{:T(128)}, f32[16,6144]{1,0:T(8,128)}, f32[16,6144]{1,0:T(8,128)}, /*index=5*/s32[]{:T(128)}, s32[]{:T(128)}) while((s32[]{:T(128)}, f32[6144]{0:T(1024)S(1)}, s32[]{:T(128)}, f32[16,6144]{1,0:T(8,128)}, f32[16,6144]{1,0:T(8,128)}, /*index=5*/s32[]{:T(128)}, ...), condition=%wide.region_1.2_spmd.clone, body=%wide.region_0.1_spmd.clone.sunk | while | flops 24580 | bytes 196717 | solution.py:31
  99.5 18.6 %gather_fusion = bf16[6144,64]{1,0:T(8,128)(2,1)S(1)} fusion(bf16[64,6144]{0,1:T(8,128)(2,1)S(1)} %copy.176, s32[6144]{0:T(1024)S(1)} %copy-done.8), kind=kCustom, calls=%fused_computation | custom fusion | bytes 1597440 | tf_op jit(solution)/shard_map/gather | solution.py:101
  118.1 2.6 fusion.79
  121.7 101.0 %all-reduce.12.cloned.1.call-done = f32[192,32,32]{2,1,0:T(8,128)} async-done(((f32[192,32,32]{2,1,0:T(8,128)}), f32[192,32,32]{2,1,0:T(8,128)}) %all-reduce.12.cloned.1.call-update) | async-done | bytes 786448 | tf_op jit(solution)/shard_map/psum | solution.py:104
  222.7 3.1 select_reduce_fusion
  225.8 2.1 multiply_reduce_fusion
  227.9 3.2 fusion.23
  231.1 3.2 fusion.4
  234.3 4.6 fusion.3
  238.9 3.8 fusion.80
  242.8 3.8 fusion.5
  246.6 4.2 fusion.6
  250.7 3.8 fusion.81
  254.6 4.0 fusion.8
  258.6 3.8 fusion.7
  262.4 4.2 fusion.82
  266.6 4.0 fusion.10
  274.5 4.7 multiply_bitcast_fusion
  279.2 17.2 %copy.179 = bf16[61,32,1152]{0,1,2:T(8,128)(2,1)} copy(bf16[61,32,1152]{2,1,0:T(8,128)(2,1)} %multiply_bitcast_fusion) | data formatting | bytes 8994816 | tf_op jit(solution)/shard_map/transpose | solution.py:109
  296.4 22.9 %copy.181 = bf16[61,32,192,6]{1,3,2,0:T(8,128)(2,1)} copy(bf16[61,32,192,6]{0,1,3,2:T(8,128)(2,1)} %bitcast.166) | data formatting | bytes 8994816 | tf_op jit(solution)/shard_map/transpose | solution.py:109
  319.3 3.7 copy.184
  322.9 1.8 copy.178
  324.8 2.1 pad_maximum_fusion
  326.8 20.6 %copy.180 = bf16[1,124,192,32]{3,0,2,1:T(2,128)(2,1)} copy(bf16[1,124,192,32]{1,3,2,0:T(8,128)(2,1)} %pad_maximum_fusion) | data formatting | bytes 3047424 | tf_op jit(solution)/shard_map/concatenate | solution.py:108
  347.4 394.6 %convert_reduce_fusion = bf16[64,192,6]{2,1,0:T(8,128)(2,1)S(1)} fusion(bf16[1,124,192,32]{3,0,2,1:T(2,128)(2,1)} %copy.180, bf16[61,32,192,6]{1,3,2,0:T(8,128)(2,1)} %copy.181), kind=kOutput, calls=%fused_computation.4 | convolution fusion | flops 287907840 | bytes 6168576 | tf_op jit(solution)/shard_map/conv_general_dilated | solution.py:110
  742.1 6.3 reshape.661
  (113 shorter events, 45.8 us)
Async XLA Ops:
  7.2 215.5 %all-reduce.12.cloned.1.call-start = ((), (), s32[]{:S(2)}) async-start(), calls=%async_computation | async-start | bytes 6291456 | tf_op jit(solution)/shard_map/psum | solution.py:104
  8.1 8.8 %collective-permute-start = (bf16[1,6144]{1,0:T(2,128)(2,1)S(1)}, bf16[1,6144]{1,0:T(2,128)(2,1)S(1)}, u32[]{:S(2)}, u32[]{:S(2)}) collective-permute-start(bf16[1,6144]{1,0:T(2,128)(2,1)S(1)} %slice.111), channel_id=1, source_target_pairs={{0,1},{1,2},{2,3},{3,4},{4,5},{5,6},{6,7},{7,8},{8,9},{9,10},{10,1... | collective-permute-start | bytes 36872 | tf_op jit(solution)/shard_map/ppermute | solution.py:17
  16.9 2.8 copy-start.2
  19.8 3.0 copy-start.3
  93.2 2.5 copy-start.4
  93.2 2.5 copy-start.5
  93.3 2.4 copy-start.6
  98.5 1.0 copy-start.8
  120.7 0.9 copy-start.7
  222.7 3.1 copy-start
  270.6 1.7 copy-start.1
  273.2 49.8 %collective-permute-start.1 = (bf16[60,6144]{1,0:T(8,128)(2,1)S(1)}, bf16[60,6144]{1,0:T(8,128)(2,1)}, u32[]{:S(2)}, u32[]{:S(2)}) collective-permute-start(bf16[60,6144]{1,0:T(8,128)(2,1)S(1)} %copy.177), channel_id=1, source_target_pairs={{1,0},{2,1},{3,2},{4,3},{5,4},{6,5},{7,6},{8,7},{9,8},{10,9},{11,1... | collective-permute-start | bytes 2211848 | tf_op jit(solution)/shard_map/ppermute | solution.py:17
Sparse Core Ops, SparseCore 0:
  120.9 101.7 all-reduce.11
where the time goes:
time: 766 us; the launch traced here: 755 us
  matrix products  442 us (58%)
  local copies, waits for them, and re-layouts  127 us (17%)
  waiting for transfers between devices  101 us (13%)
  blocking collectives  42.2 us (6%)
  other arithmetic  24.5 us (3%)
  between operations  14.6 us (2%)
    conv_general_dilated x1, matrix products, local(): lax.conv_general_dilated(extended[None], kernel, (1,), 'VALID', dimension...  395 us
    psum x1, waiting for transfers between devices, local(): covariance = lax.psum(partial_sum, 'tm') / total_t  101 us
    all_gather x2, blocking collectives, prefix(): pieces = jax.tree.map(lambda part: lax.all_gather(part, axis), value)  42.2 us
    transpose x2, local copies, waits for them, and re-layouts, local(): (templates * support[:, None, :].astype(jnp.bfloat16)).transpose(1, 2, 0)  40.1 us
    concatenate x1, local copies, waits for them, and re-layouts, local(): extended = jnp.concatenate([white, following], axis=0)  20.6 us
    gather x1, local copies, waits for them, and re-layouts, local(): grouped = stored[:, channel_ids].reshape(row_count, n_groups, NB)  18.6 us
    dynamic_slice x15, local copies, waits for them, and re-layouts, lap(): longer = join(running, jax.tree.map(lambda part: part[position], pieces))  16 us
    dot_general x4, matrix products, root_inverse(): jnp.einsum('gij,gjk->gik', middle, inverse, precision=lax.Precision.HIGHEST)  15.4 us
  transfers between devices with their start and end apart: 3, of which 1 were waited for; matrix products, arithmetic and copies ran while one was open for 7% of the time, Pallas kernels for 0%

commit v1 on v0

v1 whole, which is shorter than its diff:
```python
import functools

import jax
import jax.numpy as jnp
from jax import lax
from jax.experimental import pallas as pl
from jax.experimental.pallas import tpu as pltpu
from jax.sharding import PartitionSpec as P

NB = 32
PACK = 4
LANES = NB * PACK
STEP = 8
NS_ITERS = 4
RIDGE = 0.1
VMEM_LIMIT = 28 * 1024 * 1024
F32, BF16 = jnp.float32, jnp.bfloat16


def nt_dot(a, b):
    return lax.dot_general(a, b, (((1,), (1,)), ((), ())), preferred_element_type=F32)


def halves(a):
    high = a.astype(BF16)
    return high, (a - high.astype(F32)).astype(BF16)


def mul(a, b):
    a_high, a_low = halves(a)
    b_high, b_low = halves(b)
    right = jnp.concatenate([b_high, b_low], axis=1)
    out = jnp.dot(
        jnp.concatenate([a_high, a_low], axis=1),
        jnp.concatenate([right, right], axis=0),
        preferred_element_type=F32,
    )
    return out[:, :LANES] + out[:, LANES:]


def down(v, distance):
    zeros = jnp.zeros((distance, v.shape[1]), v.dtype)
    return jnp.concatenate([zeros, v[:-distance]], axis=0)


def up(v):
    return jnp.concatenate([v[1:], jnp.zeros((1, v.shape[1]), v.dtype)], axis=0)


def prepare_kernel(
    groups, per, rows, mine, left_ref, right_ref, left_used, right_used, order_ref, pole_ref,
    weights_ref, picks_ref, poles_ref,
):
    taps = left_ref.shape[0]
    packs = weights_ref.shape[0]
    me = mine[0]
    count = groups * per
    size = packs * rows
    row = lax.broadcasted_iota(jnp.int32, (size, 2 * LANES), 0)
    lane = lax.broadcasted_iota(jnp.int32, (size, 2 * LANES), 1)
    number = (row // rows) * PACK * per + row % rows
    real = (row % rows < PACK * per) & (number < count)
    base = ((me * count) // LANES) * LANES
    select = (real & (base + lane == me * count + number)).astype(F32).astype(BF16)
    row = lax.broadcasted_iota(jnp.int32, (size, LANES), 0)
    lane = lax.broadcasted_iota(jnp.int32, (size, LANES), 1)
    own = (row % rows) // per == lane // NB
    used = jnp.concatenate([left_used[...], right_used[...]], axis=1).astype(F32).astype(BF16)
    pad = (STEP - 1) * rows
    for c in range(packs):
        weights_ref[c, :pad, :] = jnp.zeros((pad, LANES), BF16)
        weights_ref[c, pad + taps * rows:, :] = jnp.zeros((pad, LANES), BF16)
    for s in range(taps):
        block = jnp.concatenate([left_ref[s], right_ref[s]], axis=1) * used
        spread = nt_dot(select, jnp.concatenate([block] * PACK, axis=0))
        spread = jnp.where(own, spread, 0.0).astype(BF16)
        for c in range(packs):
            weights_ref[c, pad + s * rows:pad + (s + 1) * rows, :] = spread[c * rows:(c + 1) * rows]

    length, blocks = order_ref.shape
    lane = lax.broadcasted_iota(jnp.int32, (length, blocks), 1)
    ids_lane = lax.broadcasted_iota(jnp.int32, (LANES, LANES), 1)
    for c in range(packs):
        start = me * groups + PACK * c
        block = start // 2
        ids = jnp.concatenate(
            [
                jnp.sum(jnp.where(lane == block + k, order_ref[...], 0), axis=1, keepdims=True) + length * k
                for k in range(2)
            ],
            axis=0,
        )
        pole = pole_ref[pl.ds(block // 2, 1), :]
        if groups % PACK:
            last = pole_ref.shape[0] - 1
            after = pole_ref[pl.ds(jnp.minimum(block // 2 + 1, last), 1), :]
            joined = jnp.concatenate([pole[:, length:], after[:, :length]], axis=1)
            pole = jnp.where(block % 2 == 1, joined, pole)
            ids = jnp.where(start % 2 == 1, jnp.concatenate([ids[NB:], ids[:NB]], axis=0), ids)
        pick = (ids_lane == ids).astype(F32)
        picks_ref[c] = pick.astype(BF16)
        poles_ref[c] = lax.dot_general(
            jnp.broadcast_to(pole, (8, LANES)), pick, (((1,), (1,)), ((), ())),
            precision=lax.Precision.HIGHEST, preferred_element_type=F32,
        )


def main_kernel(
    groups, rows, taps, raw_any, picks_ref, poles_ref, weights_any, out_ref,
    raw_ref, weights_ref, first, state, stored, white, total, sems,
):
    n, length, width = raw_ref.shape
    fetch_raw = pltpu.make_async_copy(raw_any, raw_ref, sems.at[0])
    fetch_weights = pltpu.make_async_copy(weights_any, weights_ref, sems.at[1])
    fetch_raw.start()
    fetch_weights.start()
    packs = range(width // LANES)
    blocks = length // STEP
    row_id = lax.broadcasted_iota(jnp.int32, (LANES, LANES), 0)
    lane_id = lax.broadcasted_iota(jnp.int32, (LANES, LANES), 1)
    same = (row_id // NB) == (lane_id // NB)
    eye = (row_id == lane_id).astype(F32)
    ones = same.astype(F32)
    poles = [jnp.broadcast_to(poles_ref[c, :1, :], (n, LANES)) for c in packs]
    gains = [0.5 * (1.0 + pole) for pole in poles]
    fetch_raw.wait()
    for c in packs:
        part = raw_ref[:, :, c * LANES:(c + 1) * LANES].reshape(n * length, LANES)
        first[c] = nt_dot(part, picks_ref[c])

    level = [jnp.zeros((n, LANES), F32) for c in packs]
    last = [down(first[c, pl.ds(length - 1, n, stride=length), :], 1) for c in packs]
    for j in range(length):
        for c in packs:
            now = first[c, pl.ds(j, n, stride=length), :]
            level[c] = poles[c] * level[c] + gains[c] * (now - last[c])
            last[c] = now
            state[c, j * n:(j + 1) * n, :] = level[c]
    incoming = []
    for c in packs:
        span, square, left = None, poles[c], length
        while left:
            if left % 2:
                span = square if span is None else span * square
            square = square * square
            left //= 2
        value, distance = level[c], 1
        while distance < n:
            value = value + span * down(value, distance)
            span = span * span
            distance *= 2
        incoming.append(down(value, 1))
    carried = list(incoming)
    for j in range(length):
        for c in packs:
            carried[c] = carried[c] * poles[c]
            stored[c, j * n:(j + 1) * n, :] = (state[c, j * n:(j + 1) * n, :] + carried[c]).astype(BF16)

    estimate, inverse, norms = [], [], []
    for c in packs:
        y = stored[c]
        gram = lax.dot_general(y, y, (((0,), (0,)), ((), ())), preferred_element_type=F32)
        cov = jnp.where(same, gram / (n * length), 0.0)
        sums = jnp.concatenate(
            [jnp.sum(cov * eye, axis=0, keepdims=True), jnp.sum(cov * cov, axis=0, keepdims=True),
             jnp.zeros((6, LANES), F32)], axis=0,
        )
        sums = jnp.dot(sums, ones, precision=lax.Precision.HIGHEST, preferred_element_type=F32)
        trace, squares = sums[0:1], sums[1:2]
        ridge = RIDGE * trace / NB
        norm = jnp.sqrt(squares + 2.0 * ridge * trace + NB * ridge * ridge)
        norms.append(norm)
        estimate.append((cov + ridge * eye) / norm)
    for repeat in range(NS_ITERS):
        if repeat == 0:
            middle = [1.5 * eye - 0.5 * estimate[c] for c in packs]
        else:
            middle = [1.5 * eye - 0.5 * mul(inverse[c], estimate[c]) for c in packs]
        if repeat < NS_ITERS - 1:
            estimate = [mul(estimate[c], middle[c]) for c in packs]
        inverse = middle if repeat == 0 else [mul(middle[c], inverse[c]) for c in packs]

    base = len(packs) * 2 * blocks
    tile = LANES // NB
    fold = ((row_id % NB) == (lane_id % NB)).astype(F32).astype(BF16)
    spread = []
    whitenings = [inverse[c] / jnp.sqrt(norms[c]) for c in packs]
    for c in packs:
        wide = jnp.dot(whitenings[c].astype(BF16), fold, preferred_element_type=F32)
        spread.append(jnp.where(lane_id // NB == row_id % tile, wide, 0.0).astype(BF16))
    tiles = NB // tile
    held = len(packs) * PACK
    to = lax.broadcasted_iota(jnp.int32, (tiles * held, held * NB), 0)
    source = lax.broadcasted_iota(jnp.int32, (tiles * held, held * NB), 1)
    gather = (source // NB == to % held) & ((source % NB) // tile == to // held)
    flat = jnp.dot(
        gather.astype(F32).astype(BF16), jnp.concatenate(spread, axis=0), preferred_element_type=F32
    ).astype(BF16)
    for seg in range(n):
        out_ref[seg, base:base + tiles * held, :] = flat
    for c in packs:
        whitening = whitenings[c]
        right = jnp.concatenate(halves(whitening), axis=1)
        for i in range(blocks):
            y = stored[c, i * STEP * n:(i + 1) * STEP * n, :]
            rows_white = nt_dot(jnp.concatenate([y, y], axis=1), right)
            for b in range(STEP):
                w = rows_white[b * n:(b + 1) * n]
                white[c, b, i * n:(i + 1) * n, :] = w.astype(BF16)
                white[c, b, (blocks + i) * n:(blocks + i + 1) * n, :] = up(w).astype(BF16)

    reach = taps + STEP - 1
    fetch_weights.wait()
    size = blocks * n
    for c in packs:
        acc = jnp.zeros((size, STEP * rows), F32)
        for u in range(0, reach, 2):
            pair = [u] if u + 1 == reach else [u, u + 1]
            acc = acc + nt_dot(
                jnp.concatenate(
                    [white[c, v % STEP, (v // STEP) * n:(v // STEP) * n + size, :] for v in pair], axis=1
                ),
                jnp.concatenate(
                    [weights_ref[c, v * rows:(v + STEP) * rows, :] for v in pair], axis=1
                ),
            )
        total[0] = acc[:, :LANES]
        total[1] = acc[:, LANES:]
        for seg in range(n):
            both = [total[h, pl.ds(seg, blocks, stride=n), :] for h in range(2)]
            out_ref[seg, c * 2 * blocks:(c + 1) * 2 * blocks, :] = jnp.concatenate(both, axis=0).astype(BF16)


def final_kernel(groups, per, rows, got_ref, scores_ref, whitening_ref, joined, wide):
    n = got_ref.shape[0]
    packs = -(-groups // PACK)
    length, columns = scores_ref.shape
    blocks = length // STEP
    base = packs * 2 * blocks
    held = packs * PACK
    tiles = (NB * NB) // LANES
    for src in range(n):
        for k in range(tiles):
            at = base + k * held
            block = got_ref[src, base:base + tiles * held, :].astype(F32) if k == 0 else block
            joined[src * groups:(src + 1) * groups, k * LANES:(k + 1) * LANES] = (
                block[k * held:k * held + groups]
            )
    step = 2 * LANES
    row_id = lax.broadcasted_iota(jnp.int32, (step, step), 0)
    lane_id = lax.broadcasted_iota(jnp.int32, (step, step), 1)
    eye = (row_id == lane_id).astype(F32).astype(BF16)
    high = step // NB
    for k in range((NB * NB) // step):
        turned = nt_dot(eye, joined[:, k * step:(k + 1) * step].astype(BF16))
        whitening_ref[k * high:(k + 1) * high] = turned.reshape(high, NB, n * groups)
    each = min(PACK, groups) * per
    lane = lax.broadcasted_iota(jnp.int32, (blocks, LANES), 1)
    pieces = [(src, c) for src in range(n) for c in range(packs)]
    tiles = columns // LANES
    for h in range(2):
        loaded = {}
        for o in range(tiles):
            outs = [None] * (STEP // 2)
            for m in range((o * LANES) // each, min(len(pieces), -(-((o + 1) * LANES) // each))):
                if m not in loaded:
                    src, c = pieces[m]
                    loaded[m] = got_ref[src, c * 2 * blocks:(c + 1) * 2 * blocks, :].astype(F32)[
                        h * blocks:(h + 1) * blocks
                    ]
                at = m * each - o * LANES
                for q in range(STEP // 2):
                    shift = (at - q * rows) % LANES
                    moved = pltpu.roll(loaded[m], shift, 1) if shift else loaded[m]
                    if outs[q] is None:
                        outs[q] = moved
                    else:
                        outs[q] = jnp.where(lane >= at, moved, outs[q])
            for q in range(STEP // 2):
                tb = STEP - 1 - (h * (STEP // 2) + q)
                wide[o, pl.ds(tb, blocks, stride=STEP), :] = outs[q]
    for o in range(tiles):
        scores_ref[:, o * LANES:(o + 1) * LANES] = wide[o].astype(BF16)


def params():
    return pltpu.CompilerParams(vmem_limit_bytes=VMEM_LIMIT)


def local(raw, pole, order, templates, support):
    length, channels = raw.shape
    n = lax.axis_size("tm")
    me = lax.axis_index("tm").astype(jnp.int32).reshape(1)
    all_groups = channels // NB
    groups = all_groups // n
    per = templates.shape[0] // all_groups
    taps = templates.shape[1]
    count = groups * per
    packs = -(-groups // PACK)
    rows = NB
    width = packs * LANES
    blocks = length // STEP

    if groups % PACK == 0:
        send = raw.reshape(length, n, width).transpose(1, 0, 2)
    else:
        pieces = [raw[:, (d * groups // 2) * 2 * NB:][:, :width] for d in range(n)]
        send = jnp.stack(pieces, axis=0)
    received = lax.all_to_all(send, "tm", 0, 0, tiled=True)

    vmem = pl.BlockSpec(memory_space=pltpu.VMEM)
    anywhere = pl.BlockSpec(memory_space=pl.ANY)
    tap_rows = (taps + 2 * (STEP - 1)) * rows
    by_lane = templates.transpose(1, 2, 0)
    used = support.T
    ends = by_lane.shape[2] // LANES - 1

    def left(s):
        return (s[0] * count) // LANES

    def right(s):
        return jnp.minimum((s[0] * count) // LANES + 1, ends)

    def whole(shape):
        return pl.BlockSpec(shape, lambda i, s: (0,) * len(shape))

    poles = pole.reshape(-1, LANES)
    shapes = [
        jax.ShapeDtypeStruct((packs, tap_rows, LANES), BF16),
        jax.ShapeDtypeStruct((packs, LANES, LANES), BF16),
        jax.ShapeDtypeStruct((packs, 8, LANES), F32),
    ]
    weights, picks, permuted = pl.pallas_call(
        functools.partial(prepare_kernel, groups, per, rows),
        out_shape=shapes,
        grid_spec=pltpu.PrefetchScalarGridSpec(
            num_scalar_prefetch=1,
            grid=(1,),
            in_specs=[
                pl.BlockSpec((taps, NB, LANES), lambda i, s: (0, 0, left(s))),
                pl.BlockSpec((taps, NB, LANES), lambda i, s: (0, 0, right(s))),
                pl.BlockSpec((NB, LANES), lambda i, s: (0, left(s))),
                pl.BlockSpec((NB, LANES), lambda i, s: (0, right(s))),
                whole(order.T.shape),
                whole(poles.shape),
            ],
            out_specs=[whole(shape.shape) for shape in shapes],
        ),
        compiler_params=params(),
        name="prepare",
    )(me, by_lane, by_lane, used, used, order.T, poles)

    total_rows = n * length
    payload = jax.ShapeDtypeStruct((n, packs * (2 * blocks + NB), LANES), BF16)
    sent = pl.pallas_call(
        functools.partial(main_kernel, groups, rows, taps),
        out_shape=payload,
        in_specs=[anywhere, vmem, vmem, anywhere],
        out_specs=vmem,
        scratch_shapes=[
            pltpu.VMEM((n, length, width), BF16),
            pltpu.VMEM((packs, tap_rows, LANES), BF16),
            pltpu.VMEM((packs, total_rows, LANES), F32),
            pltpu.VMEM((packs, total_rows, LANES), F32),
            pltpu.VMEM((packs, total_rows, LANES), BF16),
            pltpu.VMEM((packs, STEP, 2 * blocks * n, LANES), BF16),
            pltpu.VMEM((2, blocks * n, LANES), F32),
            pltpu.SemaphoreType.DMA((2,)),
        ],
        compiler_params=params(),
        name="filter_whiten_match",
    )(received, picks, permuted, weights)
    got = lax.all_to_all(sent, "tm", 0, 0, tiled=True)

    columns = all_groups * per
    scores, whitening = pl.pallas_call(
        functools.partial(final_kernel, groups, per, rows),
        out_shape=[
            jax.ShapeDtypeStruct((length, columns), BF16),
            jax.ShapeDtypeStruct((NB, NB, all_groups), F32),
        ],
        in_specs=[vmem],
        out_specs=[vmem, vmem],
        scratch_shapes=[
            pltpu.VMEM((all_groups, NB * NB), F32),
            pltpu.VMEM((columns // LANES, length, LANES), F32),
        ],
        compiler_params=params(),
        name="unpack",
    )(got)
    return scores, whitening.transpose(2, 0, 1)


def solution(mesh):
    in_specs = (P(("rec", "tm"), None), P(), P(), P(), P())
    out_specs = (P(("rec", "tm"), None), P("rec", None, None))
    return jax.shard_map(local, mesh=mesh, in_specs=in_specs, out_specs=out_specs, check_vma=False)
```

time: 766 us -> 62.5 us (0.08); the launches traced: 755 us -> 62 us
  matrix products: 442 us -> 0 us
  local copies, waits for them, and re-layouts: 127 us -> 6.81 us
  waiting for transfers between devices: 101 us -> 12.3 us
  other arithmetic: 24.5 us -> 0 us
  blocking collectives: 42.2 us -> 22.6 us
  between operations: 14.6 us -> 0.66 us
  Pallas kernels: 0 us -> 12.3 us
    conv_general_dilated x1 -> x0, matrix products: 395 us -> none  [local(): lax.conv_general_dilated(extended[None], kernel, (1,), 'VALID', dimension...]
    psum x1 -> x0, waiting for transfers between devices: 101 us -> none  [local(): covariance = lax.psum(partial_sum, 'tm') / total_t]
    dot_general x13 -> x0, matrix products: 47.1 us -> none  [the longest x4 15.4 us: root_inverse(): jnp.einsum('gij,gjk->gik', middle, inverse, precision=lax.Precision.HIGHEST)]
    all_gather x2 -> x0, blocking collectives: 42.2 us -> none  [prefix(): pieces = jax.tree.map(lambda part: lax.all_gather(part, axis), value)]
    transpose x2 -> x0, local copies, waits for them, and re-layouts: 40.1 us -> none  [local(): (templates * support[:, None, :].astype(jnp.bfloat16)).transpose(1, 2, 0)]
    all_to_all x0 -> x1, blocking collectives: none -> 22.6 us  [local(): got = lax.all_to_all(sent, 'tm', 0, 0, tiled=True)]
    concatenate x3 -> x0, local copies, waits for them, and re-layouts: 21.3 us -> none  [the longest x1 20.6 us: local(): extended = jnp.concatenate([white, following], axis=0)]
    gather x1 -> x0, local copies, waits for them, and re-layouts: 18.6 us -> none  [local(): grouped = stored[:, channel_ids].reshape(row_count, n_groups, NB)]
  transfers between devices with their start and end apart: 3 -> 1, of which waited for: 1 -> 1; matrix products, arithmetic and copies ran while one was open for 7% -> 0% of each run, Pallas kernels for 0% -> 3%
where the time goes in v1:
time: 62.5 us; the launch traced here: 62 us
  blocking collectives  22.6 us (36%)
  Pallas kernels  12.3 us (20%)
  waiting for transfers between devices  12.3 us (20%)
  starting transfers between devices  7.39 us (12%)
  local copies, waits for them, and re-layouts  6.81 us (11%)
  between operations  0.66 us (1%)
    all_to_all x1, blocking collectives, local(): got = lax.all_to_all(sent, 'tm', 0, 0, tiled=True)  22.6 us
    all_to_all x1, waiting for transfers between devices, local(): received = lax.all_to_all(send, 'tm', 0, 0, tiled=True)  12.3 us
    pallas_call x1, Pallas kernels, local(): pl.pallas_call(functools.partial(main_kernel, groups, rows, taps), out_sh...  9.16 us
    all_to_all x1, starting transfers between devices, local(): received = lax.all_to_all(send, 'tm', 0, 0, tiled=True)  7.39 us
    unnamed x8, local copies, waits for them, and re-layouts  4.67 us
    reshape x1, local copies, waits for them, and re-layouts, local(): send = raw.reshape(length, n, width).transpose(1, 0, 2)  2.13 us
    pallas_call x1, Pallas kernels, local(): pl.pallas_call(functools.partial(prepare_kernel, groups, per, rows), out_...  1.72 us
    pallas_call x1, Pallas kernels, local(): pl.pallas_call(functools.partial(final_kernel, groups, per, rows), out_sh...  1.39 us
  transfers between devices with their start and end apart: 1, of which 1 were waited for; matrix products, arithmetic and copies ran while one was open for 0% of the time, Pallas kernels for 3%

profile of v1, /device:TPU:0, one launch (start us, length us, event | category | flops | bytes accessed | tf_op | source)
XLA Modules:
  0.0 62.0 jit_solution(7588253377282343511)
XLA Ops:
  0.6 2.1 %copy.10 = bf16[8,16,8,384]{3,2,0,1:T(8,128)(2,1)} copy(bf16[8,16,8,384]{3,2,1,0:T(8,128)(2,1)} %bitcast.19) | data formatting | bytes 1572864 | tf_op jit(solution)/shard_map/reshape | solution.py:305
  2.8 7.4 %all-to-all-start = ((bf16[16,64,384]{2,1,0:T(8,128)(2,1)}), bf16[16,64,384]{2,1,0:T(8,128)(2,1)S(1)}, u32[]{:S(2)}, u32[]{:S(2)}) async-start(bf16[16,64,384]{2,1,0:T(8,128)(2,1)} %bitcast.12), calls=%async_computation | async-start | bytes 1572864 | tf_op jit(solution)/shard_map/all_to_all | solution.py:309
  10.2 0.0 copy-start
  10.2 2.3 %copy-done = bf16[1152,61,32]{0,2,1:T(8,128)(2,1)S(1)} copy-done((bf16[1152,61,32]{0,2,1:T(8,128)(2,1)S(1)}, bf16[1152,61,32]{0,2,1:T(8,128)(2,1)}, u32[]{:S(2)}) %copy-start) | copy-done | bytes 4497432
  12.4 0.0 copy-start.1
  12.4 0.9 %copy-done.1 = s32[1152,32]{0,1:T(8,128)S(1)} copy-done((s32[1152,32]{0,1:T(8,128)S(1)}, s32[1152,32]{0,1:T(8,128)}, u32[]{:S(2)}) %copy-start.1) | copy-done | bytes 147480
  13.3 0.0 copy-start.2
  13.4 0.8 %copy-done.2 = s32[96,64]{0,1:T(8,128)S(1)} copy-done((s32[96,64]{0,1:T(8,128)S(1)}, s32[96,64]{0,1:T(8,128)}, u32[]{:S(2)}) %copy-start.2) | copy-done | bytes 24600
  14.1 0.0 copy-start.3
  14.1 0.7 %copy-done.3 = f32[6144]{0:T(1024)S(1)} copy-done((f32[6144]{0:T(1024)S(1)}, f32[6144]{0:T(1024)}, u32[]{:S(2)}) %copy-start.3) | copy-done | bytes 24600
  14.8 1.7 %prepare.1 = (bf16[3,2400,128]{2,1,0:T(8,128)(2,1)S(1)}, bf16[3,128,128]{2,1,0:T(8,128)(2,1)S(1)}, f32[3,8,128]{2,1,0:T(8,128)S(1)}) custom-call(s32[1]{0:T(128)} %bitcast.1.mine, bf16[61,32,1152]{2,1,0:T(8,128)(2,1)S(1)} %bitcast.13, bf16[61,32,1152]{2,1,0:T(8,128)(2,1)S(1)} %bitcast.14, s32[32,1152]{1,0:T(8,128)S(1)} %bitcast.15, s32[32,1152]{1,0:T(8,128)S(1)} %bitcast.16, ...), custom_call_target="tpu_custom_call" | custom-call | tf_op jit(solution)/shard_map/prepare/pallas_call | solution.py:333
  16.6 12.3 %all-to-all-done.raw_any = bf16[16,64,384]{2,1,0:T(8,128)(2,1)S(1)} async-done(((bf16[16,64,384]{2,1,0:T(8,128)(2,1)}), bf16[16,64,384]{2,1,0:T(8,128)(2,1)S(1)}, u32[]{:S(2)}, u32[]{:S(2)}) %all-to-all-start) | async-done | bytes 786464 | tf_op jit(solution)/shard_map/all_to_all | solution.py:309
  28.9 9.2 %filter_whiten_match.1 = bf16[16,144,128]{2,1,0:T(8,128)(2,1)S(1)} custom-call(bf16[16,64,384]{2,1,0:T(8,128)(2,1)S(1)} %all-to-all-done.raw_any, bf16[3,128,128]{2,1,0:T(8,128)(2,1)S(1)} %get-tuple-element.7.picks_ref, f32[3,8,128]{2,1,0:T(8,128)S(1)} %get-tuple-element.8.poles_ref, bf16[3,2400,128]{2,1,0:T(8,128)(2,1)S(1)} %get-tuple-element.9.weights_any), custom_call_target="tpu_custom_call" | custom-call | tf_op jit(solution)/shard_map/filter_whiten_match/pallas_call | solution.py:355
  38.0 22.6 %all_to_all.10.got_ref = bf16[16,144,128]{2,1,0:T(8,128)(2,1)S(1)} all-to-all(bf16[16,144,128]{2,1,0:T(8,128)(2,1)S(1)} %filter_whiten_match.1), channel_id=1, replica_groups=mesh['rec'=2,'tm'=16] {'tm'}, dimensions={0} | all-to-all | bytes 1179648 | tf_op jit(solution)/shard_map/all_to_all | solution.py:373
  60.6 1.4 %unpack.1 = (bf16[64,1152]{1,0:T(8,128)(2,1)}, f32[32,32,192]{2,1,0:T(8,128)}) custom-call(bf16[16,144,128]{2,1,0:T(8,128)(2,1)S(1)} %all_to_all.10.got_ref), custom_call_target="tpu_custom_call" | custom-call | tf_op jit(solution)/shard_map/unpack/pallas_call | solution.py:376
Async XLA Ops:
  2.8 26.1 %all-to-all-start = ((bf16[16,64,384]{2,1,0:T(8,128)(2,1)}), bf16[16,64,384]{2,1,0:T(8,128)(2,1)S(1)}, u32[]{:S(2)}, u32[]{:S(2)}) async-start(bf16[16,64,384]{2,1,0:T(8,128)(2,1)} %bitcast.12), calls=%async_computation | async-start | bytes 1572864 | tf_op jit(solution)/shard_map/all_to_all | solution.py:309
  10.2 2.3 %copy-start = (bf16[1152,61,32]{0,2,1:T(8,128)(2,1)S(1)}, bf16[1152,61,32]{0,2,1:T(8,128)(2,1)}, u32[]{:S(2)}) copy-start(bf16[1152,61,32]{0,2,1:T(8,128)(2,1)} %param.8) | copy-start | bytes 13492228
  12.4 0.9 %copy-start.1 = (s32[1152,32]{0,1:T(8,128)S(1)}, s32[1152,32]{0,1:T(8,128)}, u32[]{:S(2)}) copy-start(s32[1152,32]{0,1:T(8,128)} %param.9) | copy-start | bytes 442372
  13.3 0.8 %copy-start.2 = (s32[96,64]{0,1:T(8,128)S(1)}, s32[96,64]{0,1:T(8,128)}, u32[]{:S(2)}) copy-start(s32[96,64]{0,1:T(8,128)} %param.7) | copy-start | bytes 73732
  14.1 0.7 %copy-start.3 = (f32[6144]{0:T(1024)S(1)}, f32[6144]{0:T(1024)}, u32[]{:S(2)}) copy-start(f32[6144]{0:T(1024)} %param.6) | copy-start | bytes 73732

commit v2 on v1

--- a/solution.py
+++ b/solution.py
@@ -13,7 +13,7 @@
 STEP = 8
 NS_ITERS = 4
 RIDGE = 0.1
-VMEM_LIMIT = 28 * 1024 * 1024
+MIB = 1024 * 1024
 F32, BF16 = jnp.float32, jnp.bfloat16
 
 
@@ -47,36 +47,44 @@
     return jnp.concatenate([v[1:], jnp.zeros((1, v.shape[1]), v.dtype)], axis=0)
 
 
-def prepare_kernel(
-    groups, per, rows, mine, left_ref, right_ref, left_used, right_used, order_ref, pole_ref,
-    weights_ref, picks_ref, poles_ref,
+def template_kernel(
+    groups, per, rows, mine, left_ref, right_ref, left_used, right_used, weights_ref, lined
 ):
     taps = left_ref.shape[0]
     packs = weights_ref.shape[0]
     me = mine[0]
     count = groups * per
-    size = packs * rows
-    row = lax.broadcasted_iota(jnp.int32, (size, 2 * LANES), 0)
-    lane = lax.broadcasted_iota(jnp.int32, (size, 2 * LANES), 1)
-    number = (row // rows) * PACK * per + row % rows
-    real = (row % rows < PACK * per) & (number < count)
+    lane = lax.broadcasted_iota(jnp.int32, (2 * LANES, packs * LANES), 1)
+    row = lax.broadcasted_iota(jnp.int32, (2 * LANES, packs * LANES), 0)
+    number = (lane // LANES) * PACK * per + lane % rows
+    real = (lane % rows < PACK * per) & (number < count)
     base = ((me * count) // LANES) * LANES
-    select = (real & (base + lane == me * count + number)).astype(F32).astype(BF16)
-    row = lax.broadcasted_iota(jnp.int32, (size, LANES), 0)
-    lane = lax.broadcasted_iota(jnp.int32, (size, LANES), 1)
-    own = (row % rows) // per == lane // NB
+    select = (real & (base + row == me * count + number)).astype(F32).astype(BF16)
     used = jnp.concatenate([left_used[...], right_used[...]], axis=1).astype(F32).astype(BF16)
-    pad = (STEP - 1) * rows
-    for c in range(packs):
-        weights_ref[c, :pad, :] = jnp.zeros((pad, LANES), BF16)
-        weights_ref[c, pad + taps * rows:, :] = jnp.zeros((pad, LANES), BF16)
-    for s in range(taps):
-        block = jnp.concatenate([left_ref[s], right_ref[s]], axis=1) * used
-        spread = nt_dot(select, jnp.concatenate([block] * PACK, axis=0))
-        spread = jnp.where(own, spread, 0.0).astype(BF16)
+    pad = (STEP - 1) * NB
+    lined[:pad, :] = jnp.zeros((pad, packs * LANES), BF16)
+    lined[pad + taps * NB:, :] = jnp.zeros((pad, packs * LANES), BF16)
+    for s in range(0, taps, STEP):
+        group = range(s, min(taps, s + STEP))
+        blocks = [jnp.concatenate([left_ref[t], right_ref[t]], axis=1) * used for t in group]
+        picked = jnp.dot(jnp.concatenate(blocks, axis=0), select, preferred_element_type=F32)
+        lined[pad + s * NB:pad + (s + len(group)) * NB, :] = picked.astype(BF16)
+    lane = lax.broadcasted_iota(jnp.int32, (NB, LANES), 1)
+    taken = [(lane // rows == k).astype(F32).astype(BF16) for k in range(LANES // rows)]
+    owned = [((lane % rows) // per == g).astype(F32).astype(BF16) for g in range(PACK)]
+    for v in range(weights_ref.shape[1] // LANES):
         for c in range(packs):
-            weights_ref[c, pad + s * rows:pad + (s + 1) * rows, :] = spread[c * rows:(c + 1) * rows]
-
+            block = sum(
+                lined[(v + k) * NB:(v + k + 1) * NB, c * LANES:(c + 1) * LANES] * taken[k]
+                for k in range(LANES // rows)
+            )
+            for g in range(PACK):
+                weights_ref[c, v * LANES + g * NB:v * LANES + (g + 1) * NB, :] = block * owned[g]
+
+
+def order_kernel(groups, mine, order_ref, pole_ref, picks_ref, poles_ref):
+    me = mine[0]
+    packs = picks_ref.shape[0]
     length, blocks = order_ref.shape
     lane = lax.broadcasted_iota(jnp.int32, (length, blocks), 1)
     ids_lane = lax.broadcasted_iota(jnp.int32, (LANES, LANES), 1)
@@ -113,7 +121,6 @@
     fetch_raw = pltpu.make_async_copy(raw_any, raw_ref, sems.at[0])
     fetch_weights = pltpu.make_async_copy(weights_any, weights_ref, sems.at[1])
     fetch_raw.start()
-    fetch_weights.start()
     packs = range(width // LANES)
     blocks = length // STEP
     row_id = lax.broadcasted_iota(jnp.int32, (LANES, LANES), 0)
@@ -124,6 +131,7 @@
     poles = [jnp.broadcast_to(poles_ref[c, :1, :], (n, LANES)) for c in packs]
     gains = [0.5 * (1.0 + pole) for pole in poles]
     fetch_raw.wait()
+    fetch_weights.start()
     for c in packs:
         part = raw_ref[:, :, c * LANES:(c + 1) * LANES].reshape(n * length, LANES)
         first[c] = nt_dot(part, picks_ref[c])
@@ -216,13 +224,20 @@
         acc = jnp.zeros((size, STEP * rows), F32)
         for u in range(0, reach, 2):
             pair = [u] if u + 1 == reach else [u, u + 1]
-            acc = acc + nt_dot(
+            acc = acc + jnp.dot(
                 jnp.concatenate(
                     [white[c, v % STEP, (v // STEP) * n:(v // STEP) * n + size, :] for v in pair], axis=1
                 ),
                 jnp.concatenate(
-                    [weights_ref[c, v * rows:(v + STEP) * rows, :] for v in pair], axis=1
+                    [
+                        jnp.concatenate(
+                            [weights_ref[c, w * LANES:(w + 1) * LANES, :] for w in (v, v + STEP // 2)], axis=1
+                        )
+                        for v in pair
+                    ],
+                    axis=0,
                 ),
+                preferred_element_type=F32,
             )
         total[0] = acc[:, :LANES]
         total[1] = acc[:, LANES:]
@@ -283,8 +298,8 @@
         scores_ref[:, o * LANES:(o + 1) * LANES] = wide[o].astype(BF16)
 
 
-def params():
-    return pltpu.CompilerParams(vmem_limit_bytes=VMEM_LIMIT)
+def params(mib):
+    return pltpu.CompilerParams(vmem_limit_bytes=mib * MIB)
 
 
 def local(raw, pole, order, templates, support):
@@ -310,7 +325,7 @@
 
     vmem = pl.BlockSpec(memory_space=pltpu.VMEM)
     anywhere = pl.BlockSpec(memory_space=pl.ANY)
-    tap_rows = (taps + 2 * (STEP - 1)) * rows
+    tap_rows = (taps + 2 * STEP - 2 - (LANES // rows - 1)) * LANES
     by_lane = templates.transpose(1, 2, 0)
     used = support.T
     ends = by_lane.shape[2] // LANES - 1
@@ -325,14 +340,9 @@
         return pl.BlockSpec(shape, lambda i, s: (0,) * len(shape))
 
     poles = pole.reshape(-1, LANES)
-    shapes = [
-        jax.ShapeDtypeStruct((packs, tap_rows, LANES), BF16),
-        jax.ShapeDtypeStruct((packs, LANES, LANES), BF16),
-        jax.ShapeDtypeStruct((packs, 8, LANES), F32),
-    ]
-    weights, picks, permuted = pl.pallas_call(
-        functools.partial(prepare_kernel, groups, per, rows),
-        out_shape=shapes,
+    weights = pl.pallas_call(
+        functools.partial(template_kernel, groups, per, rows),
+        out_shape=jax.ShapeDtypeStruct((packs, tap_rows, LANES), BF16),
         grid_spec=pltpu.PrefetchScalarGridSpec(
             num_scalar_prefetch=1,
             grid=(1,),
@@ -341,14 +351,24 @@
                 pl.BlockSpec((taps, NB, LANES), lambda i, s: (0, 0, right(s))),
                 pl.BlockSpec((NB, LANES), lambda i, s: (0, left(s))),
                 pl.BlockSpec((NB, LANES), lambda i, s: (0, right(s))),
-                whole(order.T.shape),
-                whole(poles.shape),
             ],
-            out_specs=[whole(shape.shape) for shape in shapes],
+            out_specs=whole((packs, tap_rows, LANES)),
+            scratch_shapes=[pltpu.VMEM(((taps + 2 * STEP - 2) * NB, width), BF16)],
         ),
-        compiler_params=params(),
-        name="prepare",
-    )(me, by_lane, by_lane, used, used, order.T, poles)
+        compiler_params=params(58),
+        name="templates",
+    )(me, by_lane, by_lane, used, used)
+    picks, permuted = pl.pallas_call(
+        functools.partial(order_kernel, groups),
+        out_shape=[
+            jax.ShapeDtypeStruct((packs, LANES, LANES), BF16),
+            jax.ShapeDtypeStruct((packs, 8, LANES), F32),
+        ],
+        in_specs=[pl.BlockSpec(memory_space=pltpu.SMEM), vmem, vmem],
+        out_specs=[vmem, vmem],
+        compiler_params=params(16),
+        name="order",
+    )(me, order.T, poles)
 
     total_rows = n * length
     payload = jax.ShapeDtypeStruct((n, packs * (2 * blocks + NB), LANES), BF16)
@@ -367,7 +387,7 @@
             pltpu.VMEM((2, blocks * n, LANES), F32),
             pltpu.SemaphoreType.DMA((2,)),
         ],
-        compiler_params=params(),
+        compiler_params=params(52),
         name="filter_whiten_match",
     )(received, picks, permuted, weights)
     got = lax.all_to_all(sent, "tm", 0, 0, tiled=True)
@@ -385,7 +405,7 @@
             pltpu.VMEM((all_groups, NB * NB), F32),
             pltpu.VMEM((columns // LANES, length, LANES), F32),
         ],
-        compiler_params=params(),
+        compiler_params=params(28),
         name="unpack",
     )(got)
     return scores, whitening.transpose(2, 0, 1)

time: 62.5 us -> 60.3 us (0.965)
  Pallas kernels: 12.3 us -> 15.6 us
  local copies, waits for them, and re-layouts: 6.81 us -> 3.62 us
  waiting for transfers between devices: 12.3 us -> 10 us
    pallas_call x1 -> x2, Pallas kernels: 1.72 us -> 7.19 us  [the longest x1 6.58 us: local(): pl.pallas_call(functools.partial(template_kernel, groups, per, rows), out...]
    unnamed x8 -> x4, local copies, waits for them, and re-layouts: 4.67 us -> 1.49 us
    all_to_all x1, waiting for transfers between devices: 12.3 us -> 10 us  [local(): received = lax.all_to_all(send, 'tm', 0, 0, tiled=True)]
    pallas_call x1, Pallas kernels: 9.16 us -> 7 us  [local(): pl.pallas_call(functools.partial(main_kernel, groups, rows, taps), out_sh...]
  transfers between devices with their start and end apart: 1 -> 1, of which waited for: 1 -> 1; matrix products, arithmetic and copies ran while one was open for 0% -> 0% of each run, Pallas kernels for 3% -> 12%
where the time goes in v2:
time: 60.3 us; the launch traced here: 59.8 us
  blocking collectives  22.6 us (37%)
  Pallas kernels  15.6 us (26%)
  waiting for transfers between devices  10 us (17%)
  starting transfers between devices  7.39 us (12%)
  local copies, waits for them, and re-layouts  3.62 us (6%)
  between operations  0.66 us (1%)
    all_to_all x1, blocking collectives, local(): got = lax.all_to_all(sent, 'tm', 0, 0, tiled=True)  22.6 us
    all_to_all x1, waiting for transfers between devices, local(): received = lax.all_to_all(send, 'tm', 0, 0, tiled=True)  10 us
    all_to_all x1, starting transfers between devices, local(): received = lax.all_to_all(send, 'tm', 0, 0, tiled=True)  7.39 us
    pallas_call x1, Pallas kernels, local(): pl.pallas_call(functools.partial(main_kernel, groups, rows, taps), out_sh...  7 us
    pallas_call x1, Pallas kernels, local(): pl.pallas_call(functools.partial(template_kernel, groups, per, rows), out...  6.58 us
    reshape x1, local copies, waits for them, and re-layouts, local(): send = raw.reshape(length, n, width).transpose(1, 0, 2)  2.13 us
    unnamed x4, local copies, waits for them, and re-layouts  1.49 us
    pallas_call x1, Pallas kernels, local(): pl.pallas_call(functools.partial(final_kernel, groups, per, rows), out_sh...  1.39 us
  transfers between devices with their start and end apart: 1, of which 1 were waited for; matrix products, arithmetic and copies ran while one was open for 0% of the time, Pallas kernels for 12%

profile of v2, /device:TPU:0, one launch (start us, length us, event | category | flops | bytes accessed | tf_op | source)
XLA Modules:
  0.0 59.8 jit_solution(586649578107511069)
XLA Ops:
  0.6 2.1 %copy.10 = bf16[8,16,8,384]{3,2,0,1:T(8,128)(2,1)} copy(bf16[8,16,8,384]{3,2,1,0:T(8,128)(2,1)} %bitcast.17) | data formatting | bytes 1572864 | tf_op jit(solution)/shard_map/reshape | solution.py:320
  2.8 7.4 %all-to-all-start = ((bf16[16,64,384]{2,1,0:T(8,128)(2,1)}), bf16[16,64,384]{2,1,0:T(8,128)(2,1)S(1)}, u32[]{:S(2)}, u32[]{:S(2)}) async-start(bf16[16,64,384]{2,1,0:T(8,128)(2,1)} %bitcast.12), calls=%async_computation | async-start | bytes 1572864 | tf_op jit(solution)/shard_map/all_to_all | solution.py:324
  10.2 0.0 copy-start
  10.2 0.7 %copy-done = s32[96,64]{0,1:T(8,128)S(1)} copy-done((s32[96,64]{0,1:T(8,128)S(1)}, s32[96,64]{0,1:T(8,128)}, u32[]{:S(2)}) %copy-start) | copy-done | bytes 24600
  10.9 0.0 copy-start.1
  10.9 0.7 %copy-done.1 = f32[6144]{0:T(1024)S(1)} copy-done((f32[6144]{0:T(1024)S(1)}, f32[6144]{0:T(1024)}, u32[]{:S(2)}) %copy-start.1) | copy-done | bytes 24600
  11.7 0.6 %order.1 = (bf16[3,128,128]{2,1,0:T(8,128)(2,1)S(1)}, f32[3,8,128]{2,1,0:T(8,128)S(1)}) custom-call(s32[1]{0:T(128)} %bitcast.1.mine, s32[64,96]{1,0:T(8,128)S(1)} %bitcast.13, f32[48,128]{1,0:T(8,128)S(1)} %bitcast.14), custom_call_target="tpu_custom_call" | custom-call | tf_op jit(solution)/shard_map/order/pallas_call | solution.py:361
  12.3 6.6 %templates.1.weights_any = bf16[3,9216,128]{2,1,0:T(8,128)(2,1)} custom-call(s32[1]{0:T(128)} %bitcast.1.mine, bf16[61,32,1152]{2,1,0:T(8,128)(2,1)} %bitcast.15, bf16[61,32,1152]{2,1,0:T(8,128)(2,1)} %bitcast.16, s32[32,1152]{1,0:T(8,128)} %bitcast.18, s32[32,1152]{1,0:T(8,128)} %bitcast.19), custom_call_target="tpu_custom_call" | custom-call | tf_op jit(solution)/shard_map/templates/pallas_call | solution.py:343
  18.9 10.0 %all-to-all-done.raw_any = bf16[16,64,384]{2,1,0:T(8,128)(2,1)S(1)} async-done(((bf16[16,64,384]{2,1,0:T(8,128)(2,1)}), bf16[16,64,384]{2,1,0:T(8,128)(2,1)S(1)}, u32[]{:S(2)}, u32[]{:S(2)}) %all-to-all-start) | async-done | bytes 786464 | tf_op jit(solution)/shard_map/all_to_all | solution.py:324
  28.9 7.0 %filter_whiten_match.1 = bf16[16,144,128]{2,1,0:T(8,128)(2,1)S(1)} custom-call(bf16[16,64,384]{2,1,0:T(8,128)(2,1)S(1)} %all-to-all-done.raw_any, bf16[3,128,128]{2,1,0:T(8,128)(2,1)S(1)} %get-tuple-element.6.picks_ref, f32[3,8,128]{2,1,0:T(8,128)S(1)} %get-tuple-element.7.poles_ref, bf16[3,9216,128]{2,1,0:T(8,128)(2,1)} %templates.1.weights_any), custom_call_target="tpu_custom_call" | custom-call | tf_op jit(solution)/shard_map/filter_whiten_match/pallas_call | solution.py:375
  35.9 22.6 %all_to_all.10.got_ref = bf16[16,144,128]{2,1,0:T(8,128)(2,1)S(1)} all-to-all(bf16[16,144,128]{2,1,0:T(8,128)(2,1)S(1)} %filter_whiten_match.1), channel_id=1, replica_groups=mesh['rec'=2,'tm'=16] {'tm'}, dimensions={0} | all-to-all | bytes 1179648 | tf_op jit(solution)/shard_map/all_to_all | solution.py:393
  58.4 1.4 %unpack.1 = (bf16[64,1152]{1,0:T(8,128)(2,1)}, f32[32,32,192]{2,1,0:T(8,128)}) custom-call(bf16[16,144,128]{2,1,0:T(8,128)(2,1)S(1)} %all_to_all.10.got_ref), custom_call_target="tpu_custom_call" | custom-call | tf_op jit(solution)/shard_map/unpack/pallas_call | solution.py:396
Async XLA Ops:
  2.8 26.1 %all-to-all-start = ((bf16[16,64,384]{2,1,0:T(8,128)(2,1)}), bf16[16,64,384]{2,1,0:T(8,128)(2,1)S(1)}, u32[]{:S(2)}, u32[]{:S(2)}) async-start(bf16[16,64,384]{2,1,0:T(8,128)(2,1)} %bitcast.12), calls=%async_computation | async-start | bytes 1572864 | tf_op jit(solution)/shard_map/all_to_all | solution.py:324
  10.2 0.8 %copy-start = (s32[96,64]{0,1:T(8,128)S(1)}, s32[96,64]{0,1:T(8,128)}, u32[]{:S(2)}) copy-start(s32[96,64]{0,1:T(8,128)} %param.7) | copy-start | bytes 73732
  10.9 0.7 %copy-start.1 = (f32[6144]{0:T(1024)S(1)}, f32[6144]{0:T(1024)}, u32[]{:S(2)}) copy-start(f32[6144]{0:T(1024)} %param.6) | copy-start | bytes 73732

commit v3 on v2

--- a/solution.py
+++ b/solution.py
@@ -45,6 +45,12 @@
 
 def up(v):
     return jnp.concatenate([v[1:], jnp.zeros((1, v.shape[1]), v.dtype)], axis=0)
+
+
+def layout(groups, width, blocks):
+    score_tiles = width // LANES
+    diagonal_at = score_tiles * blocks
+    return score_tiles, diagonal_at, -(-(diagonal_at + blocks) // 16) * 16
 
 
 def template_kernel(
@@ -82,7 +88,21 @@
                 weights_ref[c, v * LANES + g * NB:v * LANES + (g + 1) * NB, :] = block * owned[g]
 
 
-def order_kernel(groups, mine, order_ref, pole_ref, picks_ref, poles_ref):
+def order_kernel(groups, per, rows, mine, order_ref, pole_ref, picks_ref, poles_ref, places_ref, turns_ref):
+    row = lax.broadcasted_iota(jnp.int32, (places_ref.shape[0], 1), 0)
+    number = (row // (STEP * rows)) * PACK * per + row % rows
+    held = (row % rows < PACK * per) & (number < groups * per)
+    place = jnp.where(held, ((row % (STEP * rows)) // rows) * groups * per + number, -1)
+    lane = lax.broadcasted_iota(jnp.int32, places_ref.shape, 1)
+    places_ref[...] = (lane == place).astype(F32).astype(BF16)
+    row = lax.broadcasted_iota(jnp.int32, (NB * NB, 1), 0)
+    low = jnp.minimum(row // NB, row % NB)
+    high = jnp.maximum(row // NB, row % NB)
+    half = NB // 2
+    place = jnp.where(low < high, (high - half) * NB + low - half, half * NB + low)
+    place = jnp.where(low < half, low * NB + high, place)
+    lane = lax.broadcasted_iota(jnp.int32, turns_ref.shape, 1)
+    turns_ref[...] = (lane == place).astype(F32).astype(BF16)
     me = mine[0]
     packs = picks_ref.shape[0]
     length, blocks = order_ref.shape
@@ -114,12 +134,13 @@
 
 
 def main_kernel(
-    groups, rows, taps, raw_any, picks_ref, poles_ref, weights_any, out_ref,
-    raw_ref, weights_ref, first, state, stored, white, total, sems,
+    groups, rows, taps, raw_any, picks_ref, poles_ref, places_any, weights_any, out_ref,
+    raw_ref, places_ref, weights_ref, first, state, stored, white, total, sems,
 ):
     n, length, width = raw_ref.shape
     fetch_raw = pltpu.make_async_copy(raw_any, raw_ref, sems.at[0])
     fetch_weights = pltpu.make_async_copy(weights_any, weights_ref, sems.at[1])
+    fetch_places = pltpu.make_async_copy(places_any, places_ref, sems.at[2])
     fetch_raw.start()
     packs = range(width // LANES)
     blocks = length // STEP
@@ -132,6 +153,7 @@
     gains = [0.5 * (1.0 + pole) for pole in poles]
     fetch_raw.wait()
     fetch_weights.start()
+    fetch_places.start()
     for c in packs:
         part = raw_ref[:, :, c * LANES:(c + 1) * LANES].reshape(n * length, LANES)
         first[c] = nt_dot(part, picks_ref[c])
@@ -188,24 +210,39 @@
             estimate = [mul(estimate[c], middle[c]) for c in packs]
         inverse = middle if repeat == 0 else [mul(middle[c], inverse[c]) for c in packs]
 
-    base = len(packs) * 2 * blocks
-    tile = LANES // NB
-    fold = ((row_id % NB) == (lane_id % NB)).astype(F32).astype(BF16)
-    spread = []
+    score_tiles, diagonal_at, flat_at = layout(groups, places_ref.shape[1], blocks)
+    tile, half = LANES // NB, NB // 2
+    folded = row_id % NB
+    fold = jnp.concatenate([folded == lane_id % NB, folded == lane_id % NB + half], axis=1).astype(F32).astype(BF16)
+    j, k = row_id % NB, lane_id % NB
+    quarter = lane_id // NB
+    spread, diagonals = [], []
     whitenings = [inverse[c] / jnp.sqrt(norms[c]) for c in packs]
     for c in packs:
         wide = jnp.dot(whitenings[c].astype(BF16), fold, preferred_element_type=F32)
-        spread.append(jnp.where(lane_id // NB == row_id % tile, wide, 0.0).astype(BF16))
-    tiles = NB // tile
+        upper = jnp.where((j < half) & (k >= j), wide[:, :LANES], 0.0)
+        lower = jnp.where(k < j - half, wide[:, LANES:], 0.0)
+        spread.append(jnp.where(quarter == row_id % tile, upper + lower, 0.0).astype(BF16))
+        group = c * PACK + row_id // NB
+        diagonals.append(
+            jnp.where((quarter == group // 8) & (j == k), wide[:, :LANES], 0.0).astype(BF16)
+        )
+    tiles = half // tile
     held = len(packs) * PACK
     to = lax.broadcasted_iota(jnp.int32, (tiles * held, held * NB), 0)
     source = lax.broadcasted_iota(jnp.int32, (tiles * held, held * NB), 1)
-    gather = (source // NB == to % held) & ((source % NB) // tile == to // held)
+    gather = (source // NB == to % held) & ((source % half) // tile == to // held)
     flat = jnp.dot(
         gather.astype(F32).astype(BF16), jnp.concatenate(spread, axis=0), preferred_element_type=F32
     ).astype(BF16)
     for seg in range(n):
-        out_ref[seg, base:base + tiles * held, :] = flat
+        out_ref[seg, flat_at:flat_at + tiles * held, :] = flat
+    to = lax.broadcasted_iota(jnp.int32, (8, held * NB), 0)
+    source = lax.broadcasted_iota(jnp.int32, (8, held * NB), 1)
+    diagonal = jnp.dot(
+        ((source // NB) % 8 == to).astype(F32).astype(BF16), jnp.concatenate(diagonals, axis=0),
+        preferred_element_type=F32,
+    )
     for c in packs:
         whitening = whitenings[c]
         right = jnp.concatenate(halves(whitening), axis=1)
@@ -219,6 +256,7 @@
 
     reach = taps + STEP - 1
     fetch_weights.wait()
+    fetch_places.wait()
     size = blocks * n
     for c in packs:
         acc = jnp.zeros((size, STEP * rows), F32)
@@ -239,62 +277,67 @@
                 ),
                 preferred_element_type=F32,
             )
-        total[0] = acc[:, :LANES]
-        total[1] = acc[:, LANES:]
-        for seg in range(n):
-            both = [total[h, pl.ds(seg, blocks, stride=n), :] for h in range(2)]
-            out_ref[seg, c * 2 * blocks:(c + 1) * 2 * blocks, :] = jnp.concatenate(both, axis=0).astype(BF16)
-
-
-def final_kernel(groups, per, rows, got_ref, scores_ref, whitening_ref, joined, wide):
+        placed = jnp.dot(
+            acc.astype(BF16), places_ref[c * STEP * rows:(c + 1) * STEP * rows, :], preferred_element_type=F32
+        )
+        packed = placed if c == 0 else packed + placed
+    for t in range(score_tiles):
+        total[t] = packed[:, t * LANES:(t + 1) * LANES]
+    for seg in range(n):
+        parts = [total[t, pl.ds(seg, blocks, stride=n), :] for t in range(score_tiles)] + [diagonal]
+        if len(parts) % 2:
+            parts.append(jnp.zeros_like(diagonal))
+        for t in range(0, len(parts), 2):
+            both = jnp.concatenate(parts[t:t + 2], axis=0).astype(BF16)
+            out_ref[seg, t * blocks:(t + 2) * blocks, :] = both
+
+
+def final_kernel(groups, per, width, got_ref, turns_ref, scores_ref, whitening_ref, joined, wide):
     n = got_ref.shape[0]
-    packs = -(-groups // PACK)
+    held = -(-groups // PACK) * PACK
     length, columns = scores_ref.shape
     blocks = length // STEP
-    base = packs * 2 * blocks
-    held = packs * PACK
-    tiles = (NB * NB) // LANES
+    score_tiles, diagonal_at, flat_at = layout(groups, width, blocks)
+    tiles = NB // 2 * NB // LANES
+    aligned = diagonal_at // 16 * 16
+    joined[:, tiles * LANES:] = jnp.zeros((n * groups, LANES), F32)
     for src in range(n):
+        flat = got_ref[src, flat_at:flat_at + tiles * held, :].astype(F32)
         for k in range(tiles):
-            at = base + k * held
-            block = got_ref[src, base:base + tiles * held, :].astype(F32) if k == 0 else block
             joined[src * groups:(src + 1) * groups, k * LANES:(k + 1) * LANES] = (
-                block[k * held:k * held + groups]
+                flat[k * held:k * held + groups]
             )
+        ends = got_ref[src, aligned:aligned + 16, :].astype(F32)[diagonal_at - aligned:]
+        for q in range(-(-groups // 8)):
+            some = min(8, groups - 8 * q)
+            joined[src * groups + 8 * q:src * groups + 8 * q + some, tiles * LANES:tiles * LANES + NB] = (
+                ends[:some, q * NB:(q + 1) * NB]
+            )
+    entries = joined[...].astype(BF16)
     step = 2 * LANES
-    row_id = lax.broadcasted_iota(jnp.int32, (step, step), 0)
-    lane_id = lax.broadcasted_iota(jnp.int32, (step, step), 1)
-    eye = (row_id == lane_id).astype(F32).astype(BF16)
     high = step // NB
     for k in range((NB * NB) // step):
-        turned = nt_dot(eye, joined[:, k * step:(k + 1) * step].astype(BF16))
+        turned = nt_dot(turns_ref[k * step:(k + 1) * step, :], entries)
         whitening_ref[k * high:(k + 1) * high] = turned.reshape(high, NB, n * groups)
-    each = min(PACK, groups) * per
+
+    each = groups * per
     lane = lax.broadcasted_iota(jnp.int32, (blocks, LANES), 1)
-    pieces = [(src, c) for src in range(n) for c in range(packs)]
-    tiles = columns // LANES
-    for h in range(2):
-        loaded = {}
-        for o in range(tiles):
-            outs = [None] * (STEP // 2)
-            for m in range((o * LANES) // each, min(len(pieces), -(-((o + 1) * LANES) // each))):
-                if m not in loaded:
-                    src, c = pieces[m]
-                    loaded[m] = got_ref[src, c * 2 * blocks:(c + 1) * 2 * blocks, :].astype(F32)[
-                        h * blocks:(h + 1) * blocks
-                    ]
-                at = m * each - o * LANES
-                for q in range(STEP // 2):
-                    shift = (at - q * rows) % LANES
-                    moved = pltpu.roll(loaded[m], shift, 1) if shift else loaded[m]
-                    if outs[q] is None:
-                        outs[q] = moved
-                    else:
-                        outs[q] = jnp.where(lane >= at, moved, outs[q])
-            for q in range(STEP // 2):
-                tb = STEP - 1 - (h * (STEP // 2) + q)
-                wide[o, pl.ds(tb, blocks, stride=STEP), :] = outs[q]
-    for o in range(tiles):
+    for o in range(columns // LANES):
+        for tb in range(STEP):
+            out = None
+            at = o * LANES
+            while at < (o + 1) * LANES:
+                src = at // each
+                begin = tb * each + at - src * each
+                t = begin // LANES
+                stop = min((o + 1) * LANES, (src + 1) * each, at + (t + 1) * LANES - begin)
+                some = got_ref[src, t // 2 * 16:t // 2 * 16 + 16, :].astype(F32)[t % 2 * 8:t % 2 * 8 + 8]
+                shift = (at - begin) % LANES
+                moved = pltpu.roll(some, shift, 1) if shift else some
+                out = moved if out is None else jnp.where(lane >= at - o * LANES, moved, out)
+                at = stop
+            wide[o, pl.ds(STEP - 1 - tb, blocks, stride=STEP), :] = out
+    for o in range(columns // LANES):
         scores_ref[:, o * LANES:(o + 1) * LANES] = wide[o].astype(BF16)
 
 
@@ -358,56 +401,62 @@
         compiler_params=params(58),
         name="templates",
     )(me, by_lane, by_lane, used, used)
-    picks, permuted = pl.pallas_call(
-        functools.partial(order_kernel, groups),
+    score_width = -(-STEP * count // LANES) * LANES
+    _, _, flat_at = layout(groups, score_width, blocks)
+    sent_rows = -(-(flat_at + packs * PACK * NB // 2 * NB // LANES) // 16) * 16
+    picks, permuted, places, turns = pl.pallas_call(
+        functools.partial(order_kernel, groups, per, rows),
         out_shape=[
             jax.ShapeDtypeStruct((packs, LANES, LANES), BF16),
             jax.ShapeDtypeStruct((packs, 8, LANES), F32),
+            jax.ShapeDtypeStruct((packs * STEP * rows, score_width), BF16),
+            jax.ShapeDtypeStruct((NB * NB, NB // 2 * NB + LANES), BF16),
         ],
         in_specs=[pl.BlockSpec(memory_space=pltpu.SMEM), vmem, vmem],
-        out_specs=[vmem, vmem],
+        out_specs=[vmem] * 4,
         compiler_params=params(16),
         name="order",
     )(me, order.T, poles)
 
     total_rows = n * length
-    payload = jax.ShapeDtypeStruct((n, packs * (2 * blocks + NB), LANES), BF16)
+    payload = jax.ShapeDtypeStruct((n, sent_rows, LANES), BF16)
     sent = pl.pallas_call(
         functools.partial(main_kernel, groups, rows, taps),
         out_shape=payload,
-        in_specs=[anywhere, vmem, vmem, anywhere],
+        in_specs=[anywhere, vmem, vmem, anywhere, anywhere],
         out_specs=vmem,
         scratch_shapes=[
             pltpu.VMEM((n, length, width), BF16),
+            pltpu.VMEM((packs * STEP * rows, score_width), BF16),
             pltpu.VMEM((packs, tap_rows, LANES), BF16),
             pltpu.VMEM((packs, total_rows, LANES), F32),
             pltpu.VMEM((packs, total_rows, LANES), F32),
             pltpu.VMEM((packs, total_rows, LANES), BF16),
             pltpu.VMEM((packs, STEP, 2 * blocks * n, LANES), BF16),
-            pltpu.VMEM((2, blocks * n, LANES), F32),
-            pltpu.SemaphoreType.DMA((2,)),
+            pltpu.VMEM((score_width // LANES, blocks * n, LANES), F32),
+            pltpu.SemaphoreType.DMA((3,)),
         ],
         compiler_params=params(52),
         name="filter_whiten_match",
-    )(received, picks, permuted, weights)
+    )(received, picks, permuted, places, weights)
     got = lax.all_to_all(sent, "tm", 0, 0, tiled=True)
 
     columns = all_groups * per
     scores, whitening = pl.pallas_call(
-        functools.partial(final_kernel, groups, per, rows),
+        functools.partial(final_kernel, groups, per, score_width),
         out_shape=[
             jax.ShapeDtypeStruct((length, columns), BF16),
             jax.ShapeDtypeStruct((NB, NB, all_groups), F32),
         ],
-        in_specs=[vmem],
+        in_specs=[vmem, vmem],
         out_specs=[vmem, vmem],
         scratch_shapes=[
-            pltpu.VMEM((all_groups, NB * NB), F32),
+            pltpu.VMEM((all_groups, NB // 2 * NB + LANES), F32),
             pltpu.VMEM((columns // LANES, length, LANES), F32),
         ],
         compiler_params=params(28),
         name="unpack",
-    )(got)
+    )(got, turns)
     return scores, whitening.transpose(2, 0, 1)
 
 

time: 60.3 us -> 55.9 us (0.927)
  blocking collectives: 22.6 us -> 17.5 us
  waiting for transfers between devices: 10 us -> 7.96 us
  Pallas kernels: 15.6 us -> 17.3 us
  local copies, waits for them, and re-layouts: 3.62 us -> 4.59 us
    all_to_all x1, blocking collectives: 22.6 us -> 17.5 us  [local(): got = lax.all_to_all(sent, 'tm', 0, 0, tiled=True)]
    all_to_all x1, waiting for transfers between devices: 10 us -> 7.96 us  [local(): received = lax.all_to_all(send, 'tm', 0, 0, tiled=True)]
    pallas_call x2, Pallas kernels: 2 us -> 3.3 us  [the longest x1 1.72 us: local(): pl.pallas_call(functools.partial(order_kernel, groups, per, rows), out_sh...]
    unnamed x4 -> x6, local copies, waits for them, and re-layouts: 1.49 us -> 2.45 us
  transfers between devices with their start and end apart: 1 -> 1, of which waited for: 1 -> 1; matrix products, arithmetic and copies ran while one was open for 0% -> 0% of each run, Pallas kernels for 12% -> 15%
where the time goes in v3:
time: 55.9 us; the launch traced here: 55.4 us
  blocking collectives  17.5 us (31%)
  Pallas kernels  17.3 us (31%)
  waiting for transfers between devices  7.96 us (14%)
  starting transfers between devices  7.39 us (13%)
  local copies, waits for them, and re-layouts  4.59 us (8%)
  between operations  0.66 us (1%)
    all_to_all x1, blocking collectives, local(): got = lax.all_to_all(sent, 'tm', 0, 0, tiled=True)  17.5 us
    all_to_all x1, waiting for transfers between devices, local(): received = lax.all_to_all(send, 'tm', 0, 0, tiled=True)  7.96 us
    pallas_call x1, Pallas kernels, local(): pl.pallas_call(functools.partial(main_kernel, groups, rows, taps), out_sh...  7.49 us
    all_to_all x1, starting transfers between devices, local(): received = lax.all_to_all(send, 'tm', 0, 0, tiled=True)  7.39 us
    pallas_call x1, Pallas kernels, local(): pl.pallas_call(functools.partial(template_kernel, groups, per, rows), out...  6.56 us
    unnamed x6, local copies, waits for them, and re-layouts  2.45 us
    reshape x1, local copies, waits for them, and re-layouts, local(): send = raw.reshape(length, n, width).transpose(1, 0, 2)  2.14 us
    pallas_call x1, Pallas kernels, local(): pl.pallas_call(functools.partial(order_kernel, groups, per, rows), out_sh...  1.72 us
  transfers between devices with their start and end apart: 1, of which 1 were waited for; matrix products, arithmetic and copies ran while one was open for 0% of the time, Pallas kernels for 15%

profile of v3, /device:TPU:0, one launch (start us, length us, event | category | flops | bytes accessed | tf_op | source)
XLA Modules:
  0.0 55.4 jit_solution(1801326548128303328)
XLA Ops:
  0.6 2.1 %copy.10 = bf16[8,16,8,384]{3,2,0,1:T(8,128)(2,1)} copy(bf16[8,16,8,384]{3,2,1,0:T(8,128)(2,1)} %bitcast.17) | data formatting | bytes 1572864 | tf_op jit(solution)/shard_map/reshape | solution.py:363
  2.8 7.4 %all-to-all-start = ((bf16[16,64,384]{2,1,0:T(8,128)(2,1)}), bf16[16,64,384]{2,1,0:T(8,128)(2,1)S(1)}, u32[]{:S(2)}, u32[]{:S(2)}) async-start(bf16[16,64,384]{2,1,0:T(8,128)(2,1)} %bitcast.12), calls=%async_computation | async-start | bytes 1572864 | tf_op jit(solution)/shard_map/all_to_all | solution.py:367
  10.2 0.0 copy-start.1
  10.2 0.7 %copy-done.1 = s32[96,64]{0,1:T(8,128)S(1)} copy-done((s32[96,64]{0,1:T(8,128)S(1)}, s32[96,64]{0,1:T(8,128)}, u32[]{:S(2)}) %copy-start.1) | copy-done | bytes 24600
  10.9 0.0 copy-start.2
  10.9 0.7 %copy-done.2 = f32[6144]{0:T(1024)S(1)} copy-done((f32[6144]{0:T(1024)S(1)}, f32[6144]{0:T(1024)}, u32[]{:S(2)}) %copy-start.2) | copy-done | bytes 24600
  11.7 1.7 %order.1 = (bf16[3,128,128]{2,1,0:T(8,128)(2,1)S(1)}, f32[3,8,128]{2,1,0:T(8,128)S(1)}, bf16[768,640]{1,0:T(8,128)(2,1)S(1)}, bf16[1024,640]{1,0:T(8,128)(2,1)S(1)}) custom-call(s32[1]{0:T(128)} %bitcast.1.mine, s32[64,96]{1,0:T(8,128)S(1)} %bitcast.13, f32[48,128]{1,0:T(8,128)S(1)} %bitcast.14), custom_call_target="tpu_custom_call" | custom-call | tf_op jit(solution)/shard_map/order/pallas_call | solution.py:407
  13.4 0.0 copy-start
  13.4 1.0 %copy-done = bf16[768,640]{1,0:T(8,128)(2,1)} copy-done((bf16[768,640]{1,0:T(8,128)(2,1)}, bf16[768,640]{1,0:T(8,128)(2,1)S(1)}, u32[]{:S(2)}) %copy-start) | copy-done | bytes 983064
  14.3 6.6 %templates.1.weights_any = bf16[3,9216,128]{2,1,0:T(8,128)(2,1)} custom-call(s32[1]{0:T(128)} %bitcast.1.mine, bf16[61,32,1152]{2,1,0:T(8,128)(2,1)} %bitcast.15, bf16[61,32,1152]{2,1,0:T(8,128)(2,1)} %bitcast.16, s32[32,1152]{1,0:T(8,128)} %bitcast.18, s32[32,1152]{1,0:T(8,128)} %bitcast.19), custom_call_target="tpu_custom_call" | custom-call | tf_op jit(solution)/shard_map/templates/pallas_call | solution.py:386
  20.9 8.0 %all-to-all-done.raw_any = bf16[16,64,384]{2,1,0:T(8,128)(2,1)S(1)} async-done(((bf16[16,64,384]{2,1,0:T(8,128)(2,1)}), bf16[16,64,384]{2,1,0:T(8,128)(2,1)S(1)}, u32[]{:S(2)}, u32[]{:S(2)}) %all-to-all-start) | async-done | bytes 786464 | tf_op jit(solution)/shard_map/all_to_all | solution.py:367
  28.9 7.5 %filter_whiten_match.1 = bf16[16,96,128]{2,1,0:T(8,128)(2,1)S(1)} custom-call(bf16[16,64,384]{2,1,0:T(8,128)(2,1)S(1)} %all-to-all-done.raw_any, bf16[3,128,128]{2,1,0:T(8,128)(2,1)S(1)} %get-tuple-element.8.picks_ref, f32[3,8,128]{2,1,0:T(8,128)S(1)} %get-tuple-element.9.poles_ref, bf16[768,640]{1,0:T(8,128)(2,1)} %copy-done, ...), custom_call_target="tpu_custom_call" | custom-call | tf_op jit(solution)/shard_map/filter_whiten_match/pallas_call | solution.py:423
  36.4 17.5 %all_to_all.10.got_ref = bf16[16,96,128]{2,1,0:T(8,128)(2,1)S(1)} all-to-all(bf16[16,96,128]{2,1,0:T(8,128)(2,1)S(1)} %filter_whiten_match.1), channel_id=1, replica_groups=mesh['rec'=2,'tm'=16] {'tm'}, dimensions={0} | all-to-all | bytes 786432 | tf_op jit(solution)/shard_map/all_to_all | solution.py:442
  53.8 1.6 %unpack.1 = (bf16[64,1152]{1,0:T(8,128)(2,1)}, f32[32,32,192]{2,1,0:T(8,128)}) custom-call(bf16[16,96,128]{2,1,0:T(8,128)(2,1)S(1)} %all_to_all.10.got_ref, bf16[1024,640]{1,0:T(8,128)(2,1)S(1)} %get-tuple-element.11.turns_ref), custom_call_target="tpu_custom_call" | custom-call | tf_op jit(solution)/shard_map/unpack/pallas_call | solution.py:445
Async XLA Ops:
  2.8 26.1 %all-to-all-start = ((bf16[16,64,384]{2,1,0:T(8,128)(2,1)}), bf16[16,64,384]{2,1,0:T(8,128)(2,1)S(1)}, u32[]{:S(2)}, u32[]{:S(2)}) async-start(bf16[16,64,384]{2,1,0:T(8,128)(2,1)} %bitcast.12), calls=%async_computation | async-start | bytes 1572864 | tf_op jit(solution)/shard_map/all_to_all | solution.py:367
  10.2 0.8 %copy-start.1 = (s32[96,64]{0,1:T(8,128)S(1)}, s32[96,64]{0,1:T(8,128)}, u32[]{:S(2)}) copy-start(s32[96,64]{0,1:T(8,128)} %param.7) | copy-start | bytes 73732
  10.9 0.7 %copy-start.2 = (f32[6144]{0:T(1024)S(1)}, f32[6144]{0:T(1024)}, u32[]{:S(2)}) copy-start(f32[6144]{0:T(1024)} %param.6) | copy-start | bytes 73732
  13.4 1.0 %copy-start = (bf16[768,640]{1,0:T(8,128)(2,1)}, bf16[768,640]{1,0:T(8,128)(2,1)S(1)}, u32[]{:S(2)}) copy-start(bf16[768,640]{1,0:T(8,128)(2,1)S(1)} %get-tuple-element.10.places_any) | copy-start | bytes 2949124

commit v4 on v3

--- a/solution.py
+++ b/solution.py
@@ -26,16 +26,15 @@
     return high, (a - high.astype(F32)).astype(BF16)
 
 
-def mul(a, b):
-    a_high, a_low = halves(a)
+def mul(several, b):
     b_high, b_low = halves(b)
     right = jnp.concatenate([b_high, b_low], axis=1)
+    left = [jnp.concatenate(halves(a), axis=1) for a in several]
     out = jnp.dot(
-        jnp.concatenate([a_high, a_low], axis=1),
-        jnp.concatenate([right, right], axis=0),
-        preferred_element_type=F32,
+        jnp.concatenate(left, axis=0), jnp.concatenate([right, right], axis=0), preferred_element_type=F32
     )
-    return out[:, :LANES] + out[:, LANES:]
+    out = out[:, :LANES] + out[:, LANES:]
+    return [out[k * LANES:(k + 1) * LANES] for k in range(len(several))]
 
 
 def down(v, distance):
@@ -49,8 +48,8 @@
 
 def layout(groups, width, blocks):
     score_tiles = width // LANES
-    diagonal_at = score_tiles * blocks
-    return score_tiles, diagonal_at, -(-(diagonal_at + blocks) // 16) * 16
+    half_rows = (NB // 2 * NB // LANES // 2) * (-(-groups // PACK) * PACK)
+    return score_tiles * blocks, half_rows, -(-(score_tiles * blocks + half_rows) // 16) * 16
 
 
 def template_kernel(
@@ -89,6 +88,7 @@
 
 
 def order_kernel(groups, per, rows, mine, order_ref, pole_ref, picks_ref, poles_ref, places_ref, turns_ref):
+    me = mine[0]
     row = lax.broadcasted_iota(jnp.int32, (places_ref.shape[0], 1), 0)
     number = (row // (STEP * rows)) * PACK * per + row % rows
     held = (row % rows < PACK * per) & (number < groups * per)
@@ -101,9 +101,11 @@
     half = NB // 2
     place = jnp.where(low < high, (high - half) * NB + low - half, half * NB + low)
     place = jnp.where(low < half, low * NB + high, place)
+    quarter = half * NB // 2
+    swapped = jnp.where(place < quarter, place + quarter, place - quarter)
+    place = jnp.where((me % 2 == 1) & (place < half * NB), swapped, place)
     lane = lax.broadcasted_iota(jnp.int32, turns_ref.shape, 1)
     turns_ref[...] = (lane == place).astype(F32).astype(BF16)
-    me = mine[0]
     packs = picks_ref.shape[0]
     length, blocks = order_ref.shape
     lane = lax.broadcasted_iota(jnp.int32, (length, blocks), 1)
@@ -134,24 +136,21 @@
 
 
 def main_kernel(
-    groups, rows, taps, raw_any, picks_ref, poles_ref, places_any, weights_any, out_ref,
-    raw_ref, places_ref, weights_ref, first, state, stored, white, total, sems,
+    groups, rows, taps, raw_ref, picks_ref, poles_ref, places_any, weights_any, out_ref,
+    places_ref, weights_ref, first, state, stored, white, total, sems,
 ):
     n, length, width = raw_ref.shape
-    fetch_raw = pltpu.make_async_copy(raw_any, raw_ref, sems.at[0])
-    fetch_weights = pltpu.make_async_copy(weights_any, weights_ref, sems.at[1])
-    fetch_places = pltpu.make_async_copy(places_any, places_ref, sems.at[2])
-    fetch_raw.start()
+    fetch_weights = pltpu.make_async_copy(weights_any, weights_ref, sems.at[0])
+    fetch_places = pltpu.make_async_copy(places_any, places_ref, sems.at[1])
     packs = range(width // LANES)
     blocks = length // STEP
     row_id = lax.broadcasted_iota(jnp.int32, (LANES, LANES), 0)
     lane_id = lax.broadcasted_iota(jnp.int32, (LANES, LANES), 1)
     same = (row_id // NB) == (lane_id // NB)
     eye = (row_id == lane_id).astype(F32)
-    ones = same.astype(F32)
+    ones = same.astype(F32).astype(BF16)
     poles = [jnp.broadcast_to(poles_ref[c, :1, :], (n, LANES)) for c in packs]
     gains = [0.5 * (1.0 + pole) for pole in poles]
-    fetch_raw.wait()
     fetch_weights.start()
     fetch_places.start()
     for c in packs:
@@ -190,34 +189,39 @@
     for c in packs:
         y = stored[c]
         gram = lax.dot_general(y, y, (((0,), (0,)), ((), ())), preferred_element_type=F32)
-        cov = jnp.where(same, gram / (n * length), 0.0)
+        cov = jnp.where(same, gram * (1.0 / (n * length)), 0.0)
         sums = jnp.concatenate(
             [jnp.sum(cov * eye, axis=0, keepdims=True), jnp.sum(cov * cov, axis=0, keepdims=True),
              jnp.zeros((6, LANES), F32)], axis=0,
         )
-        sums = jnp.dot(sums, ones, precision=lax.Precision.HIGHEST, preferred_element_type=F32)
+        sums = jnp.dot(jnp.concatenate(halves(sums), axis=0), ones, preferred_element_type=F32)
+        sums = sums[:8] + sums[8:]
         trace, squares = sums[0:1], sums[1:2]
         ridge = RIDGE * trace / NB
         norm = jnp.sqrt(squares + 2.0 * ridge * trace + NB * ridge * ridge)
         norms.append(norm)
-        estimate.append((cov + ridge * eye) / norm)
+        estimate.append((cov + ridge * eye) * (1.0 / norm))
     for repeat in range(NS_ITERS):
         if repeat == 0:
-            middle = [1.5 * eye - 0.5 * estimate[c] for c in packs]
+            inverse = [1.5 * eye - 0.5 * estimate[c] for c in packs]
+            estimate = [mul([estimate[c]], inverse[c])[0] for c in packs]
+            continue
+        middle = [1.5 * eye - 0.5 * mul([inverse[c]], estimate[c])[0] for c in packs]
+        if repeat < NS_ITERS - 1:
+            both = [mul([inverse[c], estimate[c]], middle[c]) for c in packs]
+            inverse, estimate = [pair[0] for pair in both], [pair[1] for pair in both]
         else:
-            middle = [1.5 * eye - 0.5 * mul(inverse[c], estimate[c]) for c in packs]
-        if repeat < NS_ITERS - 1:
-            estimate = [mul(estimate[c], middle[c]) for c in packs]
-        inverse = middle if repeat == 0 else [mul(middle[c], inverse[c]) for c in packs]
-
-    score_tiles, diagonal_at, flat_at = layout(groups, places_ref.shape[1], blocks)
+            inverse = [mul([inverse[c]], middle[c])[0] for c in packs]
+
+    score_tiles = places_ref.shape[1] // LANES
+    score_rows, half_rows, sent_rows = layout(groups, places_ref.shape[1], blocks)
     tile, half = LANES // NB, NB // 2
     folded = row_id % NB
     fold = jnp.concatenate([folded == lane_id % NB, folded == lane_id % NB + half], axis=1).astype(F32).astype(BF16)
     j, k = row_id % NB, lane_id % NB
     quarter = lane_id // NB
     spread, diagonals = [], []
-    whitenings = [inverse[c] / jnp.sqrt(norms[c]) for c in packs]
+    whitenings = [inverse[c] * (1.0 / jnp.sqrt(norms[c])) for c in packs]
     for c in packs:
         wide = jnp.dot(whitenings[c].astype(BF16), fold, preferred_element_type=F32)
         upper = jnp.where((j < half) & (k >= j), wide[:, :LANES], 0.0)
@@ -225,7 +229,7 @@
         spread.append(jnp.where(quarter == row_id % tile, upper + lower, 0.0).astype(BF16))
         group = c * PACK + row_id // NB
         diagonals.append(
-            jnp.where((quarter == group // 8) & (j == k), wide[:, :LANES], 0.0).astype(BF16)
+            jnp.where((quarter == tile // 2 + group // 8) & (j == k), wide[:, :LANES], 0.0).astype(BF16)
         )
     tiles = half // tile
     held = len(packs) * PACK
@@ -234,9 +238,15 @@
     gather = (source // NB == to % held) & ((source % half) // tile == to // held)
     flat = jnp.dot(
         gather.astype(F32).astype(BF16), jnp.concatenate(spread, axis=0), preferred_element_type=F32
-    ).astype(BF16)
+    )
+    split = -(-score_rows // 16) * 16
     for seg in range(n):
-        out_ref[seg, flat_at:flat_at + tiles * held, :] = flat
+        rest = [flat[seg % 2 * half_rows + split - score_rows:(seg % 2 + 1) * half_rows]]
+        spare = sent_rows - score_rows - half_rows
+        if spare:
+            rest.append(jnp.zeros((spare, LANES), F32))
+        if sent_rows > split:
+            out_ref[seg, split:sent_rows, :] = jnp.concatenate(rest, axis=0).astype(BF16)
     to = lax.broadcasted_iota(jnp.int32, (8, held * NB), 0)
     source = lax.broadcasted_iota(jnp.int32, (8, held * NB), 1)
     diagonal = jnp.dot(
@@ -284,34 +294,36 @@
     for t in range(score_tiles):
         total[t] = packed[:, t * LANES:(t + 1) * LANES]
     for seg in range(n):
-        parts = [total[t, pl.ds(seg, blocks, stride=n), :] for t in range(score_tiles)] + [diagonal]
-        if len(parts) % 2:
-            parts.append(jnp.zeros_like(diagonal))
+        core = seg % 2
+        parts = [total[t, pl.ds(seg, blocks, stride=n), :] for t in range(score_tiles)]
+        parts[-1] = parts[-1] + diagonal
+        if split > score_rows:
+            parts.append(flat[core * half_rows:core * half_rows + split - score_rows])
         for t in range(0, len(parts), 2):
             both = jnp.concatenate(parts[t:t + 2], axis=0).astype(BF16)
             out_ref[seg, t * blocks:(t + 2) * blocks, :] = both
 
 
-def final_kernel(groups, per, width, got_ref, turns_ref, scores_ref, whitening_ref, joined, wide):
+def whitening_kernel(groups, width, got_ref, other_ref, turns_ref, whitening_ref, joined):
     n = got_ref.shape[0]
     held = -(-groups // PACK) * PACK
-    length, columns = scores_ref.shape
-    blocks = length // STEP
-    score_tiles, diagonal_at, flat_at = layout(groups, width, blocks)
-    tiles = NB // 2 * NB // LANES
-    aligned = diagonal_at // 16 * 16
-    joined[:, tiles * LANES:] = jnp.zeros((n * groups, LANES), F32)
+    score_rows, half_rows, sent_rows = layout(groups, width, STEP)
+    tiles = half_rows // held
+    start = (score_rows - 1) // 16 * 16
+    joined[:, 2 * tiles * LANES:] = jnp.zeros((n * groups, LANES), F32)
     for src in range(n):
-        flat = got_ref[src, flat_at:flat_at + tiles * held, :].astype(F32)
-        for k in range(tiles):
-            joined[src * groups:(src + 1) * groups, k * LANES:(k + 1) * LANES] = (
-                flat[k * held:k * held + groups]
-            )
-        ends = got_ref[src, aligned:aligned + 16, :].astype(F32)[diagonal_at - aligned:]
+        rows = slice(src * groups, (src + 1) * groups)
+        for ref, place in ((got_ref, 0), (other_ref, 1)):
+            block = ref[src, start:sent_rows, :].astype(F32)[score_rows - start:]
+            for k in range(tiles):
+                at = (place * tiles + k) * LANES
+                joined[rows, at:at + LANES] = block[k * held:k * held + groups]
+        ends = got_ref[src, start:start + 16, :].astype(F32)[score_rows - STEP - start:]
         for q in range(-(-groups // 8)):
             some = min(8, groups - 8 * q)
-            joined[src * groups + 8 * q:src * groups + 8 * q + some, tiles * LANES:tiles * LANES + NB] = (
-                ends[:some, q * NB:(q + 1) * NB]
+            at = (PACK // 2 + q) * NB
+            joined[src * groups + 8 * q:src * groups + 8 * q + some, 2 * tiles * LANES:2 * tiles * LANES + NB] = (
+                ends[:some, at:at + NB]
             )
     entries = joined[...].astype(BF16)
     step = 2 * LANES
@@ -320,6 +332,10 @@
         turned = nt_dot(turns_ref[k * step:(k + 1) * step, :], entries)
         whitening_ref[k * high:(k + 1) * high] = turned.reshape(high, NB, n * groups)
 
+
+def scores_kernel(groups, per, got_ref, scores_ref, wide):
+    length, columns = scores_ref.shape
+    blocks = length // STEP
     each = groups * per
     lane = lax.broadcasted_iota(jnp.int32, (blocks, LANES), 1)
     for o in range(columns // LANES):
@@ -402,8 +418,7 @@
         name="templates",
     )(me, by_lane, by_lane, used, used)
     score_width = -(-STEP * count // LANES) * LANES
-    _, _, flat_at = layout(groups, score_width, blocks)
-    sent_rows = -(-(flat_at + packs * PACK * NB // 2 * NB // LANES) // 16) * 16
+    sent_rows = layout(groups, score_width, blocks)[2]
     picks, permuted, places, turns = pl.pallas_call(
         functools.partial(order_kernel, groups, per, rows),
         out_shape=[
@@ -423,10 +438,9 @@
     sent = pl.pallas_call(
         functools.partial(main_kernel, groups, rows, taps),
         out_shape=payload,
-        in_specs=[anywhere, vmem, vmem, anywhere, anywhere],
+        in_specs=[vmem, vmem, vmem, anywhere, anywhere],
         out_specs=vmem,
         scratch_shapes=[
-            pltpu.VMEM((n, length, width), BF16),
             pltpu.VMEM((packs * STEP * rows, score_width), BF16),
             pltpu.VMEM((packs, tap_rows, LANES), BF16),
             pltpu.VMEM((packs, total_rows, LANES), F32),
@@ -434,29 +448,35 @@
             pltpu.VMEM((packs, total_rows, LANES), BF16),
             pltpu.VMEM((packs, STEP, 2 * blocks * n, LANES), BF16),
             pltpu.VMEM((score_width // LANES, blocks * n, LANES), F32),
-            pltpu.SemaphoreType.DMA((3,)),
+            pltpu.SemaphoreType.DMA((2,)),
         ],
         compiler_params=params(52),
         name="filter_whiten_match",
     )(received, picks, permuted, places, weights)
     got = lax.all_to_all(sent, "tm", 0, 0, tiled=True)
 
+    other = lax.ppermute(got, "tm", [(i, i ^ 1) for i in range(n)])
+
     columns = all_groups * per
-    scores, whitening = pl.pallas_call(
-        functools.partial(final_kernel, groups, per, score_width),
-        out_shape=[
-            jax.ShapeDtypeStruct((length, columns), BF16),
-            jax.ShapeDtypeStruct((NB, NB, all_groups), F32),
-        ],
-        in_specs=[vmem, vmem],
-        out_specs=[vmem, vmem],
-        scratch_shapes=[
-            pltpu.VMEM((all_groups, NB // 2 * NB + LANES), F32),
-            pltpu.VMEM((columns // LANES, length, LANES), F32),
-        ],
+    scores = pl.pallas_call(
+        functools.partial(scores_kernel, groups, per),
+        out_shape=jax.ShapeDtypeStruct((length, columns), BF16),
+        in_specs=[vmem],
+        out_specs=vmem,
+        scratch_shapes=[pltpu.VMEM((columns // LANES, length, LANES), F32)],
+        cost_estimate=pl.CostEstimate(flops=10**8, bytes_accessed=4 * 10**6, transcendentals=0),
         compiler_params=params(28),
-        name="unpack",
-    )(got, turns)
+        name="scores",
+    )(got)
+    whitening = pl.pallas_call(
+        functools.partial(whitening_kernel, groups, score_width),
+        out_shape=jax.ShapeDtypeStruct((NB, NB, all_groups), F32),
+        in_specs=[vmem, vmem, vmem],
+        out_specs=vmem,
+        scratch_shapes=[pltpu.VMEM((all_groups, NB // 2 * NB + LANES), F32)],
+        compiler_params=params(28),
+        name="whitening",
+    )(got, other, turns)
     return scores, whitening.transpose(2, 0, 1)
 
 

time: 55.9 us -> 55 us (0.984)
  blocking collectives: 17.5 us -> 15.3 us
  Pallas kernels: 17.3 us -> 18.1 us
    all_to_all x1, blocking collectives: 17.5 us -> 15.3 us  [local(): got = lax.all_to_all(sent, 'tm', 0, 0, tiled=True)]
    pallas_call x1 -> x2, Pallas kernels: 1.58 us -> 2.45 us  [the longest x1 1.57 us: local(): pl.pallas_call(functools.partial(whitening_kernel, groups, score_width),...]
    ppermute x0 -> x1, waiting for transfers between devices: none -> 0.65 us  [local(): other = lax.ppermute(got, 'tm', [(i, i ^ 1) for i in range(n)])]
  transfers between devices with their start and end apart: 1 -> 2, of which waited for: 1 -> 2; matrix products, arithmetic and copies ran while one was open for 0% -> 0% of each run, Pallas kernels for 15% -> 17%
where the time goes in v4:
time: 55 us; the launch traced here: 54.5 us
  Pallas kernels  18.1 us (33%)
  blocking collectives  15.3 us (28%)
  waiting for transfers between devices  8.44 us (15%)
  starting transfers between devices  7.39 us (13%)
  local copies, waits for them, and re-layouts  4.59 us (8%)
  between operations  0.66 us (1%)
    all_to_all x1, blocking collectives, local(): got = lax.all_to_all(sent, 'tm', 0, 0, tiled=True)  15.3 us
    all_to_all x1, waiting for transfers between devices, local(): received = lax.all_to_all(send, 'tm', 0, 0, tiled=True)  7.8 us
    all_to_all x1, starting transfers between devices, local(): received = lax.all_to_all(send, 'tm', 0, 0, tiled=True)  7.39 us
    pallas_call x1, Pallas kernels, local(): pl.pallas_call(functools.partial(main_kernel, groups, rows, taps), out_sh...  7.23 us
    pallas_call x1, Pallas kernels, local(): pl.pallas_call(functools.partial(template_kernel, groups, per, rows), out...  6.56 us
    unnamed x6, local copies, waits for them, and re-layouts  2.45 us
    reshape x1, local copies, waits for them, and re-layouts, local(): send = raw.reshape(length, n, width).transpose(1, 0, 2)  2.14 us
    pallas_call x1, Pallas kernels, local(): pl.pallas_call(functools.partial(order_kernel, groups, per, rows), out_sh...  1.89 us
  transfers between devices with their start and end apart: 2, of which 2 were waited for; matrix products, arithmetic and copies ran while one was open for 0% of the time, Pallas kernels for 17%

profile of v4, /device:TPU:0, one launch (start us, length us, event | category | flops | bytes accessed | tf_op | source)
XLA Modules:
  0.0 54.5 jit_solution(16051145842692800978)
XLA Ops:
  0.6 2.1 %copy.10 = bf16[8,16,8,384]{3,2,0,1:T(8,128)(2,1)} copy(bf16[8,16,8,384]{3,2,1,0:T(8,128)(2,1)} %bitcast.18) | data formatting | bytes 1572864 | tf_op jit(solution)/shard_map/reshape | solution.py:379
  2.8 7.4 %all-to-all-start = ((bf16[16,64,384]{2,1,0:T(8,128)(2,1)}), bf16[16,64,384]{2,1,0:T(8,128)(2,1)S(1)}, u32[]{:S(2)}, u32[]{:S(2)}) async-start(bf16[16,64,384]{2,1,0:T(8,128)(2,1)} %bitcast.12), calls=%async_computation | async-start | bytes 1572864 | tf_op jit(solution)/shard_map/all_to_all | solution.py:383
  10.2 0.0 copy-start.1
  10.2 0.7 %copy-done.1 = s32[96,64]{0,1:T(8,128)S(1)} copy-done((s32[96,64]{0,1:T(8,128)S(1)}, s32[96,64]{0,1:T(8,128)}, u32[]{:S(2)}) %copy-start.1) | copy-done | bytes 24600
  10.9 0.0 copy-start.2
  10.9 0.7 %copy-done.2 = f32[6144]{0:T(1024)S(1)} copy-done((f32[6144]{0:T(1024)S(1)}, f32[6144]{0:T(1024)}, u32[]{:S(2)}) %copy-start.2) | copy-done | bytes 24600
  11.7 1.9 %order.1 = (bf16[3,128,128]{2,1,0:T(8,128)(2,1)S(1)}, f32[3,8,128]{2,1,0:T(8,128)S(1)}, bf16[768,640]{1,0:T(8,128)(2,1)S(1)}, bf16[1024,640]{1,0:T(8,128)(2,1)S(1)}) custom-call(s32[1]{0:T(128)} %bitcast.1.mine, s32[64,96]{1,0:T(8,128)S(1)} %bitcast.13, f32[48,128]{1,0:T(8,128)S(1)} %bitcast.14), custom_call_target="tpu_custom_call" | custom-call | tf_op jit(solution)/shard_map/order/pallas_call | solution.py:422
  13.5 0.0 copy-start
  13.6 1.0 %copy-done = bf16[768,640]{1,0:T(8,128)(2,1)} copy-done((bf16[768,640]{1,0:T(8,128)(2,1)}, bf16[768,640]{1,0:T(8,128)(2,1)S(1)}, u32[]{:S(2)}) %copy-start) | copy-done | bytes 983064
  14.5 6.6 %templates.1.weights_any = bf16[3,9216,128]{2,1,0:T(8,128)(2,1)} custom-call(s32[1]{0:T(128)} %bitcast.1.mine, bf16[61,32,1152]{2,1,0:T(8,128)(2,1)} %bitcast.15, bf16[61,32,1152]{2,1,0:T(8,128)(2,1)} %bitcast.16, s32[32,1152]{1,0:T(8,128)} %bitcast.19, s32[32,1152]{1,0:T(8,128)} %bitcast.20), custom_call_target="tpu_custom_call" | custom-call | tf_op jit(solution)/shard_map/templates/pallas_call | solution.py:402
  21.1 7.8 %all-to-all-done.raw_ref = bf16[16,64,384]{2,1,0:T(8,128)(2,1)S(1)} async-done(((bf16[16,64,384]{2,1,0:T(8,128)(2,1)}), bf16[16,64,384]{2,1,0:T(8,128)(2,1)S(1)}, u32[]{:S(2)}, u32[]{:S(2)}) %all-to-all-start) | async-done | bytes 786464 | tf_op jit(solution)/shard_map/all_to_all | solution.py:383
  28.9 7.2 %filter_whiten_match.1 = bf16[16,64,128]{2,1,0:T(8,128)(2,1)S(1)} custom-call(bf16[16,64,384]{2,1,0:T(8,128)(2,1)S(1)} %all-to-all-done.raw_ref, bf16[3,128,128]{2,1,0:T(8,128)(2,1)S(1)} %get-tuple-element.6.picks_ref, f32[3,8,128]{2,1,0:T(8,128)S(1)} %get-tuple-element.7.poles_ref, bf16[768,640]{1,0:T(8,128)(2,1)} %copy-done, ...), custom_call_target="tpu_custom_call" | custom-call | tf_op jit(solution)/shard_map/filter_whiten_match/pallas_call | solution.py:438
  36.1 15.3 %all_to_all.10.got_ref = bf16[16,64,128]{2,1,0:T(8,128)(2,1)S(1)} all-to-all(bf16[16,64,128]{2,1,0:T(8,128)(2,1)S(1)} %filter_whiten_match.1), channel_id=1, replica_groups=mesh['rec'=2,'tm'=16] {'tm'}, dimensions={0} | all-to-all | bytes 524288 | tf_op jit(solution)/shard_map/all_to_all | solution.py:456
  51.4 0.0 collective-permute-start
  51.4 0.9 %scores.1 = bf16[64,1152]{1,0:T(8,128)(2,1)} custom-call(bf16[16,64,128]{2,1,0:T(8,128)(2,1)S(1)} %all_to_all.10.got_ref), custom_call_target="tpu_custom_call" | custom-call | flops 100000000 | bytes 4000000 | tf_op jit(solution)/shard_map/scores/pallas_call | solution.py:461
  52.3 0.6 %collective-permute-done.other_ref = bf16[16,64,128]{2,1,0:T(8,128)(2,1)S(1)} collective-permute-done((bf16[16,64,128]{2,1,0:T(8,128)(2,1)S(1)}, bf16[16,64,128]{2,1,0:T(8,128)(2,1)S(1)}, u32[]{:S(2)}, u32[]{:S(2)}) %collective-permute-start) | collective-permute-done | bytes 262176 | tf_op jit(solution)/shard_map/ppermute | solution.py:458
  53.0 1.6 %whitening.1 = f32[32,32,192]{2,1,0:T(8,128)} custom-call(bf16[16,64,128]{2,1,0:T(8,128)(2,1)S(1)} %all_to_all.10.got_ref, bf16[16,64,128]{2,1,0:T(8,128)(2,1)S(1)} %collective-permute-done.other_ref, bf16[1024,640]{1,0:T(8,128)(2,1)S(1)} %get-tuple-element.9.turns_ref), custom_call_target="tpu_custom_call" | custom-call | tf_op jit(solution)/shard_map/whitening/pallas_call | solution.py:471
Async XLA Ops:
  2.8 26.1 %all-to-all-start = ((bf16[16,64,384]{2,1,0:T(8,128)(2,1)}), bf16[16,64,384]{2,1,0:T(8,128)(2,1)S(1)}, u32[]{:S(2)}, u32[]{:S(2)}) async-start(bf16[16,64,384]{2,1,0:T(8,128)(2,1)} %bitcast.12), calls=%async_computation | async-start | bytes 1572864 | tf_op jit(solution)/shard_map/all_to_all | solution.py:383
  10.2 0.8 %copy-start.1 = (s32[96,64]{0,1:T(8,128)S(1)}, s32[96,64]{0,1:T(8,128)}, u32[]{:S(2)}) copy-start(s32[96,64]{0,1:T(8,128)} %param.7) | copy-start | bytes 73732
  10.9 0.7 %copy-start.2 = (f32[6144]{0:T(1024)S(1)}, f32[6144]{0:T(1024)}, u32[]{:S(2)}) copy-start(f32[6144]{0:T(1024)} %param.6) | copy-start | bytes 73732
  13.5 1.0 %copy-start = (bf16[768,640]{1,0:T(8,128)(2,1)}, bf16[768,640]{1,0:T(8,128)(2,1)S(1)}, u32[]{:S(2)}) copy-start(bf16[768,640]{1,0:T(8,128)(2,1)S(1)} %get-tuple-element.8.places_any) | copy-start | bytes 2949124
  51.4 1.5 %collective-permute-start = (bf16[16,64,128]{2,1,0:T(8,128)(2,1)S(1)}, bf16[16,64,128]{2,1,0:T(8,128)(2,1)S(1)}, u32[]{:S(2)}, u32[]{:S(2)}) collective-permute-start(bf16[16,64,128]{2,1,0:T(8,128)(2,1)S(1)} %all_to_all.10.got_ref), channel_id=1, source_target_pairs={{0,1},{1,0},{2,3},{3,2},{4,5},{5,4},{6,7},{7,6},{8,9},{9,8},{10,11... | collective-permute-start | bytes 786440 | tf_op jit(solution)/shard_map/ppermute | solution.py:458

commit v5 on v4

--- a/solution.py
+++ b/solution.py
@@ -144,6 +144,7 @@
     fetch_places = pltpu.make_async_copy(places_any, places_ref, sems.at[1])
     packs = range(width // LANES)
     blocks = length // STEP
+    pitch = length + 8
     row_id = lax.broadcasted_iota(jnp.int32, (LANES, LANES), 0)
     lane_id = lax.broadcasted_iota(jnp.int32, (LANES, LANES), 1)
     same = (row_id // NB) == (lane_id // NB)
@@ -155,13 +156,15 @@
     fetch_places.start()
     for c in packs:
         part = raw_ref[:, :, c * LANES:(c + 1) * LANES].reshape(n * length, LANES)
-        first[c] = nt_dot(part, picks_ref[c])
+        picked = nt_dot(part, picks_ref[c])
+        for seg in range(n):
+            first[c, seg * pitch:seg * pitch + length, :] = picked[seg * length:(seg + 1) * length]
 
     level = [jnp.zeros((n, LANES), F32) for c in packs]
-    last = [down(first[c, pl.ds(length - 1, n, stride=length), :], 1) for c in packs]
+    last = [down(first[c, pl.ds(length - 1, n, stride=pitch), :], 1) for c in packs]
     for j in range(length):
         for c in packs:
-            now = first[c, pl.ds(j, n, stride=length), :]
+            now = first[c, pl.ds(j, n, stride=pitch), :]
             level[c] = poles[c] * level[c] + gains[c] * (now - last[c])
             last[c] = now
             state[c, j * n:(j + 1) * n, :] = level[c]
@@ -443,7 +446,7 @@
         scratch_shapes=[
             pltpu.VMEM((packs * STEP * rows, score_width), BF16),
             pltpu.VMEM((packs, tap_rows, LANES), BF16),
-            pltpu.VMEM((packs, total_rows, LANES), F32),
+            pltpu.VMEM((packs, total_rows + 8 * n, LANES), F32),
             pltpu.VMEM((packs, total_rows, LANES), F32),
             pltpu.VMEM((packs, total_rows, LANES), BF16),
             pltpu.VMEM((packs, STEP, 2 * blocks * n, LANES), BF16),

time: 55 us -> 54.2 us (0.985)
  Pallas kernels: 18.1 us -> 17.3 us
    pallas_call x1, Pallas kernels: 7.23 us -> 6.43 us  [local(): pl.pallas_call(functools.partial(main_kernel, groups, rows, taps), out_sh...]
where the time goes in v5:
time: 54.2 us; the launch traced here: 53.7 us
  Pallas kernels  17.3 us (32%)
  blocking collectives  15.3 us (28%)
  waiting for transfers between devices  8.44 us (16%)
  starting transfers between devices  7.39 us (14%)
  local copies, waits for them, and re-layouts  4.59 us (8%)
  between operations  0.66 us (1%)
    all_to_all x1, blocking collectives, local(): got = lax.all_to_all(sent, 'tm', 0, 0, tiled=True)  15.3 us
    all_to_all x1, waiting for transfers between devices, local(): received = lax.all_to_all(send, 'tm', 0, 0, tiled=True)  7.8 us
    all_to_all x1, starting transfers between devices, local(): received = lax.all_to_all(send, 'tm', 0, 0, tiled=True)  7.39 us
    pallas_call x1, Pallas kernels, local(): pl.pallas_call(functools.partial(template_kernel, groups, per, rows), out...  6.56 us
    pallas_call x1, Pallas kernels, local(): pl.pallas_call(functools.partial(main_kernel, groups, rows, taps), out_sh...  6.43 us
    unnamed x6, local copies, waits for them, and re-layouts  2.45 us
    reshape x1, local copies, waits for them, and re-layouts, local(): send = raw.reshape(length, n, width).transpose(1, 0, 2)  2.14 us
    pallas_call x1, Pallas kernels, local(): pl.pallas_call(functools.partial(order_kernel, groups, per, rows), out_sh...  1.89 us
  transfers between devices with their start and end apart: 2, of which 2 were waited for; matrix products, arithmetic and copies ran while one was open for 0% of the time, Pallas kernels for 17%

profile of v5, /device:TPU:0, one launch (start us, length us, event | category | flops | bytes accessed | tf_op | source)
XLA Modules:
  0.0 53.7 jit_solution(14482553423471294711)
XLA Ops:
  0.6 2.1 %copy.10 = bf16[8,16,8,384]{3,2,0,1:T(8,128)(2,1)} copy(bf16[8,16,8,384]{3,2,1,0:T(8,128)(2,1)} %bitcast.18) | data formatting | bytes 1572864 | tf_op jit(solution)/shard_map/reshape | solution.py:382
  2.8 7.4 %all-to-all-start = ((bf16[16,64,384]{2,1,0:T(8,128)(2,1)}), bf16[16,64,384]{2,1,0:T(8,128)(2,1)S(1)}, u32[]{:S(2)}, u32[]{:S(2)}) async-start(bf16[16,64,384]{2,1,0:T(8,128)(2,1)} %bitcast.12), calls=%async_computation | async-start | bytes 1572864 | tf_op jit(solution)/shard_map/all_to_all | solution.py:386
  10.2 0.0 copy-start.1
  10.2 0.7 %copy-done.1 = s32[96,64]{0,1:T(8,128)S(1)} copy-done((s32[96,64]{0,1:T(8,128)S(1)}, s32[96,64]{0,1:T(8,128)}, u32[]{:S(2)}) %copy-start.1) | copy-done | bytes 24600
  10.9 0.0 copy-start.2
  10.9 0.7 %copy-done.2 = f32[6144]{0:T(1024)S(1)} copy-done((f32[6144]{0:T(1024)S(1)}, f32[6144]{0:T(1024)}, u32[]{:S(2)}) %copy-start.2) | copy-done | bytes 24600
  11.7 1.9 %order.1 = (bf16[3,128,128]{2,1,0:T(8,128)(2,1)S(1)}, f32[3,8,128]{2,1,0:T(8,128)S(1)}, bf16[768,640]{1,0:T(8,128)(2,1)S(1)}, bf16[1024,640]{1,0:T(8,128)(2,1)S(1)}) custom-call(s32[1]{0:T(128)} %bitcast.1.mine, s32[64,96]{1,0:T(8,128)S(1)} %bitcast.13, f32[48,128]{1,0:T(8,128)S(1)} %bitcast.14), custom_call_target="tpu_custom_call" | custom-call | tf_op jit(solution)/shard_map/order/pallas_call | solution.py:425
  13.5 0.0 copy-start
  13.6 1.0 %copy-done = bf16[768,640]{1,0:T(8,128)(2,1)} copy-done((bf16[768,640]{1,0:T(8,128)(2,1)}, bf16[768,640]{1,0:T(8,128)(2,1)S(1)}, u32[]{:S(2)}) %copy-start) | copy-done | bytes 983064
  14.5 6.6 %templates.1.weights_any = bf16[3,9216,128]{2,1,0:T(8,128)(2,1)} custom-call(s32[1]{0:T(128)} %bitcast.1.mine, bf16[61,32,1152]{2,1,0:T(8,128)(2,1)} %bitcast.15, bf16[61,32,1152]{2,1,0:T(8,128)(2,1)} %bitcast.16, s32[32,1152]{1,0:T(8,128)} %bitcast.19, s32[32,1152]{1,0:T(8,128)} %bitcast.20), custom_call_target="tpu_custom_call" | custom-call | tf_op jit(solution)/shard_map/templates/pallas_call | solution.py:405
  21.1 7.8 %all-to-all-done.raw_ref = bf16[16,64,384]{2,1,0:T(8,128)(2,1)S(1)} async-done(((bf16[16,64,384]{2,1,0:T(8,128)(2,1)}), bf16[16,64,384]{2,1,0:T(8,128)(2,1)S(1)}, u32[]{:S(2)}, u32[]{:S(2)}) %all-to-all-start) | async-done | bytes 786464 | tf_op jit(solution)/shard_map/all_to_all | solution.py:386
  28.9 6.4 %filter_whiten_match.1 = bf16[16,64,128]{2,1,0:T(8,128)(2,1)S(1)} custom-call(bf16[16,64,384]{2,1,0:T(8,128)(2,1)S(1)} %all-to-all-done.raw_ref, bf16[3,128,128]{2,1,0:T(8,128)(2,1)S(1)} %get-tuple-element.6.picks_ref, f32[3,8,128]{2,1,0:T(8,128)S(1)} %get-tuple-element.7.poles_ref, bf16[768,640]{1,0:T(8,128)(2,1)} %copy-done, ...), custom_call_target="tpu_custom_call" | custom-call | tf_op jit(solution)/shard_map/filter_whiten_match/pallas_call | solution.py:441
  35.3 15.3 %all_to_all.10.got_ref = bf16[16,64,128]{2,1,0:T(8,128)(2,1)S(1)} all-to-all(bf16[16,64,128]{2,1,0:T(8,128)(2,1)S(1)} %filter_whiten_match.1), channel_id=1, replica_groups=mesh['rec'=2,'tm'=16] {'tm'}, dimensions={0} | all-to-all | bytes 524288 | tf_op jit(solution)/shard_map/all_to_all | solution.py:459
  50.6 0.0 collective-permute-start
  50.6 0.9 %scores.1 = bf16[64,1152]{1,0:T(8,128)(2,1)} custom-call(bf16[16,64,128]{2,1,0:T(8,128)(2,1)S(1)} %all_to_all.10.got_ref), custom_call_target="tpu_custom_call" | custom-call | flops 100000000 | bytes 4000000 | tf_op jit(solution)/shard_map/scores/pallas_call | solution.py:464
  51.5 0.6 %collective-permute-done.other_ref = bf16[16,64,128]{2,1,0:T(8,128)(2,1)S(1)} collective-permute-done((bf16[16,64,128]{2,1,0:T(8,128)(2,1)S(1)}, bf16[16,64,128]{2,1,0:T(8,128)(2,1)S(1)}, u32[]{:S(2)}, u32[]{:S(2)}) %collective-permute-start) | collective-permute-done | bytes 262176 | tf_op jit(solution)/shard_map/ppermute | solution.py:461
  52.2 1.6 %whitening.1 = f32[32,32,192]{2,1,0:T(8,128)} custom-call(bf16[16,64,128]{2,1,0:T(8,128)(2,1)S(1)} %all_to_all.10.got_ref, bf16[16,64,128]{2,1,0:T(8,128)(2,1)S(1)} %collective-permute-done.other_ref, bf16[1024,640]{1,0:T(8,128)(2,1)S(1)} %get-tuple-element.9.turns_ref), custom_call_target="tpu_custom_call" | custom-call | tf_op jit(solution)/shard_map/whitening/pallas_call | solution.py:474
Async XLA Ops:
  2.8 26.1 %all-to-all-start = ((bf16[16,64,384]{2,1,0:T(8,128)(2,1)}), bf16[16,64,384]{2,1,0:T(8,128)(2,1)S(1)}, u32[]{:S(2)}, u32[]{:S(2)}) async-start(bf16[16,64,384]{2,1,0:T(8,128)(2,1)} %bitcast.12), calls=%async_computation | async-start | bytes 1572864 | tf_op jit(solution)/shard_map/all_to_all | solution.py:386
  10.2 0.8 %copy-start.1 = (s32[96,64]{0,1:T(8,128)S(1)}, s32[96,64]{0,1:T(8,128)}, u32[]{:S(2)}) copy-start(s32[96,64]{0,1:T(8,128)} %param.7) | copy-start | bytes 73732
  10.9 0.7 %copy-start.2 = (f32[6144]{0:T(1024)S(1)}, f32[6144]{0:T(1024)}, u32[]{:S(2)}) copy-start(f32[6144]{0:T(1024)} %param.6) | copy-start | bytes 73732
  13.5 1.0 %copy-start = (bf16[768,640]{1,0:T(8,128)(2,1)}, bf16[768,640]{1,0:T(8,128)(2,1)S(1)}, u32[]{:S(2)}) copy-start(bf16[768,640]{1,0:T(8,128)(2,1)S(1)} %get-tuple-element.8.places_any) | copy-start | bytes 2949124
  50.6 1.5 %collective-permute-start = (bf16[16,64,128]{2,1,0:T(8,128)(2,1)S(1)}, bf16[16,64,128]{2,1,0:T(8,128)(2,1)S(1)}, u32[]{:S(2)}, u32[]{:S(2)}) collective-permute-start(bf16[16,64,128]{2,1,0:T(8,128)(2,1)S(1)} %all_to_all.10.got_ref), channel_id=1, source_target_pairs={{0,1},{1,0},{2,3},{3,2},{4,5},{5,4},{6,7},{7,6},{8,9},{9,8},{10,11... | collective-permute-start | bytes 786440 | tf_op jit(solution)/shard_map/ppermute | solution.py:461

commit v6 on v5

--- a/solution.py
+++ b/solution.py
@@ -294,11 +294,13 @@
             acc.astype(BF16), places_ref[c * STEP * rows:(c + 1) * STEP * rows, :], preferred_element_type=F32
         )
         packed = placed if c == 0 else packed + placed
+    apart = n + 8
     for t in range(score_tiles):
-        total[t] = packed[:, t * LANES:(t + 1) * LANES]
+        for i in range(blocks):
+            total[t, i * apart:i * apart + n, :] = packed[i * n:(i + 1) * n, t * LANES:(t + 1) * LANES]
     for seg in range(n):
         core = seg % 2
-        parts = [total[t, pl.ds(seg, blocks, stride=n), :] for t in range(score_tiles)]
+        parts = [total[t, pl.ds(seg, blocks, stride=apart), :] for t in range(score_tiles)]
         parts[-1] = parts[-1] + diagonal
         if split > score_rows:
             parts.append(flat[core * half_rows:core * half_rows + split - score_rows])
@@ -450,7 +452,7 @@
             pltpu.VMEM((packs, total_rows, LANES), F32),
             pltpu.VMEM((packs, total_rows, LANES), BF16),
             pltpu.VMEM((packs, STEP, 2 * blocks * n, LANES), BF16),
-            pltpu.VMEM((score_width // LANES, blocks * n, LANES), F32),
+            pltpu.VMEM((score_width // LANES, blocks * (n + 8), LANES), F32),
             pltpu.SemaphoreType.DMA((2,)),
         ],
         compiler_params=params(52),

time: 54.2 us -> 54.1 us (level)
  no operation moved by 1% of the time
where the time goes in v6:
time: 54.1 us; the launch traced here: 53.7 us
  Pallas kernels  17.3 us (32%)
  blocking collectives  15.3 us (28%)
  waiting for transfers between devices  8.44 us (16%)
  starting transfers between devices  7.39 us (14%)
  local copies, waits for them, and re-layouts  4.59 us (8%)
  between operations  0.66 us (1%)
    all_to_all x1, blocking collectives, local(): got = lax.all_to_all(sent, 'tm', 0, 0, tiled=True)  15.3 us
    all_to_all x1, waiting for transfers between devices, local(): received = lax.all_to_all(send, 'tm', 0, 0, tiled=True)  7.8 us
    all_to_all x1, starting transfers between devices, local(): received = lax.all_to_all(send, 'tm', 0, 0, tiled=True)  7.39 us
    pallas_call x1, Pallas kernels, local(): pl.pallas_call(functools.partial(template_kernel, groups, per, rows), out...  6.56 us
    pallas_call x1, Pallas kernels, local(): pl.pallas_call(functools.partial(main_kernel, groups, rows, taps), out_sh...  6.38 us
    unnamed x6, local copies, waits for them, and re-layouts  2.45 us
    reshape x1, local copies, waits for them, and re-layouts, local(): send = raw.reshape(length, n, width).transpose(1, 0, 2)  2.14 us
    pallas_call x1, Pallas kernels, local(): pl.pallas_call(functools.partial(order_kernel, groups, per, rows), out_sh...  1.89 us
  transfers between devices with their start and end apart: 2, of which 2 were waited for; matrix products, arithmetic and copies ran while one was open for 0% of the time, Pallas kernels for 17%

profile of v6, /device:TPU:0, one launch (start us, length us, event | category | flops | bytes accessed | tf_op | source)
XLA Modules:
  0.0 53.7 jit_solution(184659523913486120)
XLA Ops:
  0.6 2.1 %copy.10 = bf16[8,16,8,384]{3,2,0,1:T(8,128)(2,1)} copy(bf16[8,16,8,384]{3,2,1,0:T(8,128)(2,1)} %bitcast.18) | data formatting | bytes 1572864 | tf_op jit(solution)/shard_map/reshape | solution.py:384
  2.8 7.4 %all-to-all-start = ((bf16[16,64,384]{2,1,0:T(8,128)(2,1)}), bf16[16,64,384]{2,1,0:T(8,128)(2,1)S(1)}, u32[]{:S(2)}, u32[]{:S(2)}) async-start(bf16[16,64,384]{2,1,0:T(8,128)(2,1)} %bitcast.12), calls=%async_computation | async-start | bytes 1572864 | tf_op jit(solution)/shard_map/all_to_all | solution.py:388
  10.2 0.0 copy-start.1
  10.2 0.7 %copy-done.1 = s32[96,64]{0,1:T(8,128)S(1)} copy-done((s32[96,64]{0,1:T(8,128)S(1)}, s32[96,64]{0,1:T(8,128)}, u32[]{:S(2)}) %copy-start.1) | copy-done | bytes 24600
  10.9 0.0 copy-start.2
  10.9 0.7 %copy-done.2 = f32[6144]{0:T(1024)S(1)} copy-done((f32[6144]{0:T(1024)S(1)}, f32[6144]{0:T(1024)}, u32[]{:S(2)}) %copy-start.2) | copy-done | bytes 24600
  11.7 1.9 %order.1 = (bf16[3,128,128]{2,1,0:T(8,128)(2,1)S(1)}, f32[3,8,128]{2,1,0:T(8,128)S(1)}, bf16[768,640]{1,0:T(8,128)(2,1)S(1)}, bf16[1024,640]{1,0:T(8,128)(2,1)S(1)}) custom-call(s32[1]{0:T(128)} %bitcast.1.mine, s32[64,96]{1,0:T(8,128)S(1)} %bitcast.13, f32[48,128]{1,0:T(8,128)S(1)} %bitcast.14), custom_call_target="tpu_custom_call" | custom-call | tf_op jit(solution)/shard_map/order/pallas_call | solution.py:427
  13.5 0.0 copy-start
  13.6 1.0 %copy-done = bf16[768,640]{1,0:T(8,128)(2,1)} copy-done((bf16[768,640]{1,0:T(8,128)(2,1)}, bf16[768,640]{1,0:T(8,128)(2,1)S(1)}, u32[]{:S(2)}) %copy-start) | copy-done | bytes 983064
  14.5 6.6 %templates.1.weights_any = bf16[3,9216,128]{2,1,0:T(8,128)(2,1)} custom-call(s32[1]{0:T(128)} %bitcast.1.mine, bf16[61,32,1152]{2,1,0:T(8,128)(2,1)} %bitcast.15, bf16[61,32,1152]{2,1,0:T(8,128)(2,1)} %bitcast.16, s32[32,1152]{1,0:T(8,128)} %bitcast.19, s32[32,1152]{1,0:T(8,128)} %bitcast.20), custom_call_target="tpu_custom_call" | custom-call | tf_op jit(solution)/shard_map/templates/pallas_call | solution.py:407
  21.1 7.8 %all-to-all-done.raw_ref = bf16[16,64,384]{2,1,0:T(8,128)(2,1)S(1)} async-done(((bf16[16,64,384]{2,1,0:T(8,128)(2,1)}), bf16[16,64,384]{2,1,0:T(8,128)(2,1)S(1)}, u32[]{:S(2)}, u32[]{:S(2)}) %all-to-all-start) | async-done | bytes 786464 | tf_op jit(solution)/shard_map/all_to_all | solution.py:388
  28.9 6.4 %filter_whiten_match.1 = bf16[16,64,128]{2,1,0:T(8,128)(2,1)S(1)} custom-call(bf16[16,64,384]{2,1,0:T(8,128)(2,1)S(1)} %all-to-all-done.raw_ref, bf16[3,128,128]{2,1,0:T(8,128)(2,1)S(1)} %get-tuple-element.6.picks_ref, f32[3,8,128]{2,1,0:T(8,128)S(1)} %get-tuple-element.7.poles_ref, bf16[768,640]{1,0:T(8,128)(2,1)} %copy-done, ...), custom_call_target="tpu_custom_call" | custom-call | tf_op jit(solution)/shard_map/filter_whiten_match/pallas_call | solution.py:443
  35.3 15.3 %all_to_all.10.got_ref = bf16[16,64,128]{2,1,0:T(8,128)(2,1)S(1)} all-to-all(bf16[16,64,128]{2,1,0:T(8,128)(2,1)S(1)} %filter_whiten_match.1), channel_id=1, replica_groups=mesh['rec'=2,'tm'=16] {'tm'}, dimensions={0} | all-to-all | bytes 524288 | tf_op jit(solution)/shard_map/all_to_all | solution.py:461
  50.6 0.0 collective-permute-start
  50.6 0.9 %scores.1 = bf16[64,1152]{1,0:T(8,128)(2,1)} custom-call(bf16[16,64,128]{2,1,0:T(8,128)(2,1)S(1)} %all_to_all.10.got_ref), custom_call_target="tpu_custom_call" | custom-call | flops 100000000 | bytes 4000000 | tf_op jit(solution)/shard_map/scores/pallas_call | solution.py:466
  51.5 0.6 %collective-permute-done.other_ref = bf16[16,64,128]{2,1,0:T(8,128)(2,1)S(1)} collective-permute-done((bf16[16,64,128]{2,1,0:T(8,128)(2,1)S(1)}, bf16[16,64,128]{2,1,0:T(8,128)(2,1)S(1)}, u32[]{:S(2)}, u32[]{:S(2)}) %collective-permute-start) | collective-permute-done | bytes 262176 | tf_op jit(solution)/shard_map/ppermute | solution.py:463
  52.1 1.6 %whitening.1 = f32[32,32,192]{2,1,0:T(8,128)} custom-call(bf16[16,64,128]{2,1,0:T(8,128)(2,1)S(1)} %all_to_all.10.got_ref, bf16[16,64,128]{2,1,0:T(8,128)(2,1)S(1)} %collective-permute-done.other_ref, bf16[1024,640]{1,0:T(8,128)(2,1)S(1)} %get-tuple-element.9.turns_ref), custom_call_target="tpu_custom_call" | custom-call | tf_op jit(solution)/shard_map/whitening/pallas_call | solution.py:476
Async XLA Ops:
  2.8 26.1 %all-to-all-start = ((bf16[16,64,384]{2,1,0:T(8,128)(2,1)}), bf16[16,64,384]{2,1,0:T(8,128)(2,1)S(1)}, u32[]{:S(2)}, u32[]{:S(2)}) async-start(bf16[16,64,384]{2,1,0:T(8,128)(2,1)} %bitcast.12), calls=%async_computation | async-start | bytes 1572864 | tf_op jit(solution)/shard_map/all_to_all | solution.py:388
  10.2 0.8 %copy-start.1 = (s32[96,64]{0,1:T(8,128)S(1)}, s32[96,64]{0,1:T(8,128)}, u32[]{:S(2)}) copy-start(s32[96,64]{0,1:T(8,128)} %param.7) | copy-start | bytes 73732
  10.9 0.7 %copy-start.2 = (f32[6144]{0:T(1024)S(1)}, f32[6144]{0:T(1024)}, u32[]{:S(2)}) copy-start(f32[6144]{0:T(1024)} %param.6) | copy-start | bytes 73732
  13.5 1.0 %copy-start = (bf16[768,640]{1,0:T(8,128)(2,1)}, bf16[768,640]{1,0:T(8,128)(2,1)S(1)}, u32[]{:S(2)}) copy-start(bf16[768,640]{1,0:T(8,128)(2,1)S(1)} %get-tuple-element.8.places_any) | copy-start | bytes 2949124
  50.6 1.5 %collective-permute-start = (bf16[16,64,128]{2,1,0:T(8,128)(2,1)S(1)}, bf16[16,64,128]{2,1,0:T(8,128)(2,1)S(1)}, u32[]{:S(2)}, u32[]{:S(2)}) collective-permute-start(bf16[16,64,128]{2,1,0:T(8,128)(2,1)S(1)} %all_to_all.10.got_ref), channel_id=1, source_target_pairs={{0,1},{1,0},{2,3},{3,2},{4,5},{5,4},{6,7},{7,6},{8,9},{9,8},{10,11... | collective-permute-start | bytes 786440 | tf_op jit(solution)/shard_map/ppermute | solution.py:463
